TPU v7x, 32 devices: a whole 2x2x4 slice. The times are simulated.
32 devices in a mesh: erow: 4 (over x, core), ecol: 8 (over z, y).
Axes of the slice: x: 2, y: 2, z: 4, core: 2. Of those that a mesh axis runs over, the one named last changes fastest.
Arguments:
- tokens: bfloat16 [256, 7168], P(('erow', 'ecol')), may hold values from -6 to 6
- routes: int32 [256, 4], P(('erow', 'ecol')), may hold values from 0 to 7, all different within a row; in each aligned block of 8 rows (0 to 7, 8 to 15, ...) at most 4 rows name the same one
- gate_probs: bfloat16 [256, 4], P(('erow', 'ecol')), may hold values from 0.049804688 to 0.5
- cotangent: bfloat16 [256, 7168], P(('erow', 'ecol')), may hold values from -0.625 to 0.625
- w_gate_up: bfloat16 [8, 7168, 2, 2048], P('ecol', 'erow'), may hold values from -0.0625 to 0.0625
- w_down: bfloat16 [8, 2048, 7168], P('ecol', None, 'erow'), may hold values from -0.125 to 0.125
Outputs:
- layer_out: bfloat16 [256, 7168], P(('erow', 'ecol'))
- grad_tokens: bfloat16 [256, 7168], P(('erow', 'ecol'))
- grad_probs: float32 [256, 4], P(('erow', 'ecol'))
- grad_gate_up: bfloat16 [8, 7168, 2, 2048], P('ecol', 'erow')
- grad_down: bfloat16 [8, 2048, 7168], P('ecol', None, 'erow')
Inputs may be any that keep to these rules, and one draw needn't show every extreme that they name: `routes`: each row names 4 different experts; among the 8 rows of one device no expert is named more than 4 times, and in some device's rows an expert is named exactly 4 times.
All inputs are finite; a program needn't handle non-finite values.
Results may differ from a plain program's by a relative error of at most 0.039.
Values may be sent and summed in bfloat16 or wider, within the bound.
No kernel may reach another device: no remote copies, remote signals or barrier semaphores. Data moves between devices by JAX's collectives and lax.ppermute only.
A program may use at most 128 MiB of HBM per device.

v0:
```python
import jax
import jax.numpy as jnp
from jax import lax
from jax.sharding import PartitionSpec as P


def send_rows(place_flat, slot_probs, tokens, cotangent, n_row, experts, capacity):
    token_count = tokens.shape[0]
    weight_slice = tokens.shape[1] // n_row
    token_parts = tokens.reshape(token_count, n_row, weight_slice)
    cot_parts = cotangent.reshape(token_count, n_row, weight_slice)
    x_out = (
        jnp.einsum("ts,trd->rsd", place_flat, token_parts, preferred_element_type=jnp.float32)
        .astype(jnp.bfloat16)
        .reshape(n_row * experts, capacity, weight_slice)
    )
    cot_out = (
        jnp.einsum("ts,trd->rsd", place_flat, cot_parts, preferred_element_type=jnp.float32)
        .astype(jnp.bfloat16)
        .reshape(n_row * experts, capacity, weight_slice)
    )
    prob_out = jnp.broadcast_to(
        slot_probs[None, :, :, None], (n_row, experts, capacity, 1)
    ).reshape(n_row * experts, capacity, 1)
    x_in, cot_in, prob_in = (
        lax.all_to_all(x_out, ("erow", "ecol"), split_axis=0, concat_axis=0, tiled=True),
        lax.all_to_all(cot_out, ("erow", "ecol"), split_axis=0, concat_axis=0, tiled=True),
        lax.all_to_all(prob_out, ("erow", "ecol"), split_axis=0, concat_axis=0, tiled=True),
    )
    return (x_in.reshape(-1, weight_slice), cot_in.reshape(-1, weight_slice), prob_in.reshape(-1))


def return_values(row_values, place_flat, n_row, experts, capacity):
    weight_slice = row_values.shape[1]
    returned = lax.all_to_all(
        row_values.reshape(n_row * experts, capacity, weight_slice),
        ("erow", "ecol"),
        split_axis=0,
        concat_axis=0,
        tiled=True,
    )
    summed = jnp.einsum(
        "ts,rsd->trd",
        place_flat,
        returned.reshape(n_row, experts * capacity, weight_slice),
        preferred_element_type=jnp.float32,
    )
    return summed.reshape(place_flat.shape[0], n_row * weight_slice)


def return_grads(grad_rows, dprob_rows, place_flat, n_row, experts, capacity):
    weight_slice = grad_rows.shape[1]
    returned, returned_prob = (
        lax.all_to_all(
            grad_rows.reshape(n_row * experts, capacity, weight_slice),
            ("erow", "ecol"),
            split_axis=0,
            concat_axis=0,
            tiled=True,
        ),
        lax.all_to_all(
            dprob_rows.reshape(n_row * experts, capacity, 1),
            ("erow", "ecol"),
            split_axis=0,
            concat_axis=0,
            tiled=True,
        ),
    )
    summed = jnp.einsum(
        "ts,rsd->trd",
        place_flat,
        returned.reshape(n_row, experts * capacity, weight_slice),
        preferred_element_type=jnp.float32,
    )
    slot_dprob = jnp.sum(
        returned_prob.astype(jnp.float32).reshape(n_row, experts, capacity), axis=0
    )
    return (summed.reshape(place_flat.shape[0], n_row * weight_slice), slot_dprob)


def reduce_parts(partial_term):
    return lax.psum(partial_term.astype(jnp.bfloat16), "erow").astype(jnp.float32)


def on_device(tokens, routes, gate_probs, cotangent, w_gate_up, w_down):
    n_row = lax.axis_size("erow")
    experts = lax.axis_size("ecol")
    token_count = tokens.shape[0]
    capacity = token_count // 2
    chosen = routes[:, :, None] == jnp.arange(experts, dtype=jnp.int32)[None, None, :]
    member = jnp.sum(chosen.astype(jnp.int32), axis=1)
    prior_result = jnp.cumsum(member, axis=0) - member
    placed = (member[:, :, None] == 1) & (
        prior_result[:, :, None] == jnp.arange(capacity, dtype=jnp.int32)[None, None, :]
    )
    placed = placed.astype(jnp.bfloat16)
    place_flat = placed.reshape(token_count, experts * capacity)
    probs_te = jnp.sum(
        jnp.where(chosen, gate_probs[:, :, None], jnp.zeros((), jnp.bfloat16)), axis=1
    )
    slot_probs = jnp.einsum(
        "tec,te->ec", placed, probs_te, preferred_element_type=jnp.float32
    ).astype(jnp.bfloat16)
    x_rows, cot_rows, prob_rows = send_rows(
        place_flat, slot_probs, tokens, cotangent, n_row, experts, capacity
    )
    prob_f32 = prob_rows.astype(jnp.float32)
    w_in = w_gate_up[0]
    w_out = w_down[0]
    partial_value = jnp.einsum("rd,dgf->rgf", x_rows, w_in, preferred_element_type=jnp.float32)
    pre_sums = reduce_parts(partial_value)
    gate_pre = pre_sums[:, 0, :]
    up_pre = pre_sums[:, 1, :]
    sigmoid_gate = jax.nn.sigmoid(gate_pre)
    activated = gate_pre * sigmoid_gate
    hidden = (activated * up_pre).astype(jnp.bfloat16)
    expert_out = jnp.dot(hidden, w_out, preferred_element_type=jnp.float32)
    contrib = (prob_f32[:, None] * expert_out).astype(jnp.bfloat16)
    layer_out = return_values(contrib, place_flat, n_row, experts, capacity).astype(jnp.bfloat16)
    cot_f32 = cot_rows.astype(jnp.float32)
    scaled_cotangent = (prob_f32[:, None] * cot_f32).astype(jnp.bfloat16)
    dprob_rows = jnp.sum(cot_f32 * expert_out, axis=1, keepdims=True).astype(jnp.bfloat16)
    hidden_term = jnp.einsum(
        "rd,fd->rf", scaled_cotangent, w_out, preferred_element_type=jnp.float32
    )
    hidden_gradient = reduce_parts(hidden_term[:, None, :])[:, 0, :]
    grad_gate = hidden_gradient * up_pre * sigmoid_gate * (1.0 + gate_pre * (1.0 - sigmoid_gate))
    grad_up = hidden_gradient * activated
    grad_pre = jnp.stack([grad_gate, grad_up], axis=1).astype(jnp.bfloat16)
    grad_rows = jnp.einsum(
        "rgf,dgf->rd", grad_pre, w_in, preferred_element_type=jnp.float32
    ).astype(jnp.bfloat16)
    grad_gate_up = jnp.einsum(
        "rd,rgf->dgf", x_rows, grad_pre, preferred_element_type=jnp.float32
    ).astype(jnp.bfloat16)[None]
    grad_down = jnp.einsum(
        "rf,rd->fd", hidden, scaled_cotangent, preferred_element_type=jnp.float32
    ).astype(jnp.bfloat16)[None]
    token_grads, slot_dprob = return_grads(
        grad_rows, dprob_rows, place_flat, n_row, experts, capacity
    )
    grad_tokens = token_grads.astype(jnp.bfloat16)
    dprob_te = jnp.sum(placed.astype(jnp.float32) * slot_dprob[None, :, :], axis=2)
    grad_probs = jnp.sum(jnp.where(chosen, dprob_te[:, None, :], 0.0), axis=2)
    return (layer_out, grad_tokens, grad_probs, grad_gate_up, grad_down)


def solution(mesh):
    placed = (
        P(("erow", "ecol"), None),
        P(("erow", "ecol"), None),
        P(("erow", "ecol"), None),
        P(("erow", "ecol"), None),
        P("ecol", "erow", None, None),
        P("ecol", None, "erow"),
    )
    return jax.shard_map(
        on_device,
        mesh=mesh,
        in_specs=placed,
        out_specs=(
            P(("erow", "ecol"), None),
            P(("erow", "ecol"), None),
            P(("erow", "ecol"), None),
            P("ecol", "erow", None, None),
            P("ecol", None, "erow"),
        ),
        check_vma=False,
    )
```

profile of v0, /device:TPU:0, one launch (start us, length us, event | category | flops | bytes accessed | tf_op | source)
XLA Modules:
  0.0 215.6 jit_solution(16788405577855961778)
XLA Ops:
  7.2 0.8 convert_reduce_fusion
  10.0 7.3 %all-to-all-start = ((bf16[32,4,1]{1,2,0:T(2,128)(2,1)}), bf16[32,4,1]{1,2,0:T(2,128)(2,1)S(1)}, u32[]{:S(2)}, u32[]{:S(2)}) async-start(bf16[32,4,1]{1,2,0:T(2,128)(2,1)} %copy.80), calls=%async_computation | async-start | bytes 32768 | tf_op jit(solution)/shard_map/all_to_all | solution.py:28
  17.6 0.9 reshape.229
  18.5 5.9 %all-to-all-done = bf16[32,4,1]{1,2,0:T(2,128)(2,1)S(1)} async-done(((bf16[32,4,1]{1,2,0:T(2,128)(2,1)}), bf16[32,4,1]{1,2,0:T(2,128)(2,1)S(1)}, u32[]{:S(2)}, u32[]{:S(2)}) %all-to-all-start) | async-done | bytes 288 | tf_op jit(solution)/shard_map/all_to_all | solution.py:28
  24.4 2.6 %all-to-all-start.3 = ((bf16[32,4,1792]{2,1,0:T(4,128)(2,1)}), bf16[32,4,1792]{2,1,0:T(4,128)(2,1)S(1)}, u32[]{:S(2)}, u32[]{:S(2)}) async-start(bf16[32,4,1792]{2,1,0:T(4,128)(2,1)} %reshape.229), calls=%async_computation.3 | async-start | bytes 917504 | tf_op jit(solution)/shard_map/all_to_all | solution.py:27
  27.0 1.1 fusion.21
  28.1 0.9 reshape.224
  29.0 12.9 %all-to-all-done.3 = bf16[32,4,1792]{2,1,0:T(4,128)(2,1)S(1)} async-done(((bf16[32,4,1792]{2,1,0:T(4,128)(2,1)}), bf16[32,4,1792]{2,1,0:T(4,128)(2,1)S(1)}, u32[]{:S(2)}, u32[]{:S(2)}) %all-to-all-start.3) | async-done | bytes 458784 | tf_op jit(solution)/shard_map/all_to_all | solution.py:27
  41.9 3.3 %all-to-all-start.1 = ((bf16[32,4,1792]{2,1,0:T(4,128)(2,1)}), bf16[32,4,1792]{2,1,0:T(4,128)(2,1)}, u32[]{:S(2)}, u32[]{:S(2)}) async-start(bf16[32,4,1792]{2,1,0:T(4,128)(2,1)} %reshape.224), calls=%async_computation.1 | async-start | bytes 917504 | tf_op jit(solution)/shard_map/all_to_all | solution.py:26
  45.6 0.9 convert_element_type.134
  46.5 13.7 %all-to-all-done.1 = bf16[32,4,1792]{2,1,0:T(4,128)(2,1)} async-done(((bf16[32,4,1792]{2,1,0:T(4,128)(2,1)}), bf16[32,4,1792]{2,1,0:T(4,128)(2,1)}, u32[]{:S(2)}, u32[]{:S(2)}) %all-to-all-start.1) | async-done | bytes 458784 | tf_op jit(solution)/shard_map/all_to_all | solution.py:26
  60.2 2.0 reshape.242
  62.2 15.3 %fusion.9 = bf16[128,2,2048]{2,0,1:T(8,128)(2,1)} fusion(bf16[128,1792,1]{1,0,2:T(8,128)(2,1)} %reshape.242, bf16[1792,2,2048]{2,1,0:T(2,128)(2,1)} %bitcast.78), kind=kOutput, calls=%fused_computation.13 | convolution fusion | flops 1879572480 | bytes 16187392 | tf_op jit(solution)/shard_map/rd,dgf->rgf/dot_general | solution.py:110
  77.6 3.3 %fusion.23 = bf16[128,1,2048]{2,0,1:T(8,128)(2,1)} fusion(bf16[128,1792]{1,0:T(8,128)(2,1)S(1)} %copy-done.3, bf16[1,2048,1792]{2,1,0:T(8,128)(2,1)S(1)} %bitcast.67), kind=kOutput, calls=%fused_computation.21 | convolution fusion | flops 939786240 | bytes 8323072 | tf_op jit(solution)/shard_map/rd,fd->rf/dot_general | solution.py:123
  81.1 1.1 reshape.236
  82.2 39.5 %all-reduce.3.cloned.1.call-done = (bf16[128,2,2048]{2,0,1:T(8,128)(2,1)}, bf16[128,1,2048]{2,0,1:T(8,128)(2,1)}) async-done(((bf16[128,2,2048]{2,0,1:T(8,128)(2,1)}, bf16[128,1,2048]{2,0,1:T(8,128)(2,1)}), (bf16[128,2,2048]{2,0,1:T(8,128)(2,1)}, bf16[128,1,2048]{2,0,1:T(8,128)(2,1)})) %all-reduce.3.cloned.1.call-update) | async-done | bytes 1572880 | tf_op jit(solution)/shard_map/psum | solution.py:82
  121.7 1.5 convert_element_type.123
  123.1 1.7 fusion.28
  124.9 4.5 %multiply_reduce_fusion = (bf16[128]{0:T(256)(128)(2,1)S(1)}, bf16[128,1792]{1,0:T(8,128)(2,1)S(1)}) fusion(f32[128,1792]{1,0:T(8,128)S(1)} %reshape.236, f32[128]{0:T(128)S(1)} %reshape.234, bf16[128,2048]{1,0:T(8,128)(2,1)S(1)} %get-tuple-element.41, bf16[1,2048,1792]{2,1,0:T(8,128)(2,1)} %param.11), kind=kOutput, calls=%fused_computation.32 | convolution fusion | flops 940441472 | bytes 9241344 | tf_op jit(solution)/shard_map/dot_general | solution.py:117
  130.1 4.6 %all-to-all-start.5 = ((bf16[32,4,1]{1,2,0:T(2,128)(2,1)}), bf16[32,4,1]{1,2,0:T(2,128)(2,1)S(1)}, u32[]{:S(2)}, u32[]{:S(2)}) async-start(bf16[32,4,1]{1,2,0:T(2,128)(2,1)} %convert_element_type.151), calls=%async_computation.5 | async-start | bytes 32768 | tf_op jit(solution)/shard_map/all_to_all | solution.py:61
  134.8 0.9 reshape.226
  135.6 6.2 %all-to-all-done.5 = bf16[32,4,1]{1,2,0:T(2,128)(2,1)S(1)} async-done(((bf16[32,4,1]{1,2,0:T(2,128)(2,1)}), bf16[32,4,1]{1,2,0:T(2,128)(2,1)S(1)}, u32[]{:S(2)}, u32[]{:S(2)}) %all-to-all-start.5) | async-done | bytes 288 | tf_op jit(solution)/shard_map/all_to_all | solution.py:61
  141.8 2.6 %all-to-all-start.2 = ((bf16[32,4,1792]{2,1,0:T(4,128)(2,1)}), bf16[32,4,1792]{2,1,0:T(4,128)(2,1)S(1)}, u32[]{:S(2)}, u32[]{:S(2)}) async-start(bf16[32,4,1792]{2,1,0:T(4,128)(2,1)} %reshape.226), calls=%async_computation.2 | async-start | bytes 917504 | tf_op jit(solution)/shard_map/all_to_all | solution.py:35
  144.4 13.3 %fusion.15 = bf16[128,1792]{1,0:T(8,128)(2,1)S(1)} fusion(bf16[1792,2,2048]{2,1,0:T(2,128)(2,1)} %bitcast.79, bf16[128,1,2048]{2,0,1:T(8,128)(2,1)S(1)} %get-tuple-element.40, bf16[128,1,2048]{2,0,1:T(8,128)(2,1)S(1)} %get-tuple-element.39), kind=kOutput, calls=%fused_computation.15 | convolution fusion | flops 1879801856 | bytes 16187392 | tf_op jit(solution)/shard_map/rgf,dgf->rd/dot_general | solution.py:130
  157.8 0.9 reshape.230
  159.4 5.1 %all-to-all-start.4 = ((bf16[32,4,1792]{2,1,0:T(4,128)(2,1)}), bf16[32,4,1792]{2,1,0:T(4,128)(2,1)S(1)}, u32[]{:S(2)}, u32[]{:S(2)}) async-start(bf16[32,4,1792]{2,1,0:T(4,128)(2,1)} %reshape.230), calls=%async_computation.4 | async-start | bytes 917504 | tf_op jit(solution)/shard_map/all_to_all | solution.py:54
  164.5 1.1 reshape.225
  165.6 7.3 %convert_bitcast_fusion = bf16[1,1792,2,2048]{3,1,2,0:T(8,128)(2,1)} fusion(bf16[128,1,2048]{2,0,1:T(8,128)(2,1)S(1)} %get-tuple-element.40, bf16[128,1,2048]{2,0,1:T(8,128)(2,1)S(1)} %get-tuple-element.39, bf16[128,1792]{1,0:T(8,128)(2,1)S(1)} %reshape.225), kind=kOutput, calls=%fused_computation | convolution fusion | flops 1888485376 | bytes 16187392 | tf_op jit(solution)/shard_map/rd,rgf->dgf/dot_general | solution.py:133
  172.9 27.4 %copy.94 = bf16[1,1792,2,2048]{3,2,1,0:T(2,128)(2,1)} copy(bf16[1,1792,2,2048]{3,1,2,0:T(8,128)(2,1)} %convert_bitcast_fusion) | data formatting | bytes 29360128
  200.3 5.2 %fusion.8 = bf16[1,2048,1792]{2,1,0:T(8,128)(2,1)} fusion(bf16[128,2048]{1,0:T(8,128)(2,1)S(1)} %get-tuple-element.41, bf16[128,1792]{1,0:T(8,128)(2,1)S(1)} %copy-done.4), kind=kOutput, calls=%fused_computation.12 | convolution fusion | flops 943194112 | bytes 8323072 | tf_op jit(solution)/shard_map/rf,rd->fd/dot_general | solution.py:136
  207.0 0.9 convolution_convert_fusion.1
  207.8 0.9 convolution_convert_fusion
  (51 shorter events, 5.7 us)
Async XLA Ops:
  7.2 10.2 %copy-start = (bf16[8,7168]{1,0:T(8,128)(2,1)S(1)}, bf16[8,7168]{1,0:T(8,128)(2,1)}, u32[]{:S(2)}) copy-start(bf16[8,7168]{1,0:T(8,128)(2,1)} %param.9) | copy-start | bytes 344068
  10.0 14.3 %all-to-all-start = ((bf16[32,4,1]{1,2,0:T(2,128)(2,1)}), bf16[32,4,1]{1,2,0:T(2,128)(2,1)S(1)}, u32[]{:S(2)}, u32[]{:S(2)}) async-start(bf16[32,4,1]{1,2,0:T(2,128)(2,1)} %copy.80), calls=%async_computation | async-start | bytes 32768 | tf_op jit(solution)/shard_map/all_to_all | solution.py:28
  24.4 17.6 %all-to-all-start.3 = ((bf16[32,4,1792]{2,1,0:T(4,128)(2,1)}), bf16[32,4,1792]{2,1,0:T(4,128)(2,1)S(1)}, u32[]{:S(2)}, u32[]{:S(2)}) async-start(bf16[32,4,1792]{2,1,0:T(4,128)(2,1)} %reshape.229), calls=%async_computation.3 | async-start | bytes 917504 | tf_op jit(solution)/shard_map/all_to_all | solution.py:27
  41.9 4.5 %copy-start.2 = (bf16[32,4,1792]{2,1,0:T(4,128)(2,1)}, bf16[32,4,1792]{2,1,0:T(4,128)(2,1)S(1)}, u32[]{:S(2)}) copy-start(bf16[32,4,1792]{2,1,0:T(4,128)(2,1)S(1)} %all-to-all-done.3) | copy-start | bytes 1376260
  41.9 18.3 %all-to-all-start.1 = ((bf16[32,4,1792]{2,1,0:T(4,128)(2,1)}), bf16[32,4,1792]{2,1,0:T(4,128)(2,1)}, u32[]{:S(2)}, u32[]{:S(2)}) async-start(bf16[32,4,1792]{2,1,0:T(4,128)(2,1)} %reshape.224), calls=%async_computation.1 | async-start | bytes 917504 | tf_op jit(solution)/shard_map/all_to_all | solution.py:26
  45.3 76.4 %all-reduce.3.cloned.1.call-start = ((), (), s32[]{:S(2)}) async-start(), calls=%async_computation.6 | async-start | bytes 3145728 | tf_op jit(solution)/shard_map/psum | solution.py:82
  60.2 17.4 %slice-start = ((s8[7340032]{0:T(1024)(128)(4,1)}), s8[3145728]{0:T(1024)(128)(4,1)S(1)}, s32[]{:S(2)}) async-start(s8[7340032]{0:T(1024)(128)(4,1)} %bitcast.66), calls=%async_computation.7 | async-start | bytes 6291456
  62.2 15.4 %slice-start.1 = ((s8[7340032]{0:T(1024)(128)(4,1)}), s8[4194304]{0:T(1024)(128)(4,1)S(1)}, s32[]{:S(2)}) async-start(s8[7340032]{0:T(1024)(128)(4,1)} %bitcast.66), calls=%async_computation.8 | async-start | bytes 8388608
  62.2 15.4 %copy-start.3 = (bf16[128,1792]{1,0:T(8,128)(2,1)S(1)}, bf16[128,1792]{1,0:T(8,128)(2,1)}, u32[]{:S(2)}) copy-start(bf16[128,1792]{1,0:T(8,128)(2,1)} %convert_element_type.134) | copy-start | bytes 1376260
  130.1 11.7 %all-to-all-start.5 = ((bf16[32,4,1]{1,2,0:T(2,128)(2,1)}), bf16[32,4,1]{1,2,0:T(2,128)(2,1)S(1)}, u32[]{:S(2)}, u32[]{:S(2)}) async-start(bf16[32,4,1]{1,2,0:T(2,128)(2,1)} %convert_element_type.151), calls=%async_computation.5 | async-start | bytes 32768 | tf_op jit(solution)/shard_map/all_to_all | solution.py:61
  141.8 17.6 %all-to-all-start.2 = ((bf16[32,4,1792]{2,1,0:T(4,128)(2,1)}), bf16[32,4,1792]{2,1,0:T(4,128)(2,1)S(1)}, u32[]{:S(2)}, u32[]{:S(2)}) async-start(bf16[32,4,1792]{2,1,0:T(4,128)(2,1)} %reshape.226), calls=%async_computation.2 | async-start | bytes 917504 | tf_op jit(solution)/shard_map/all_to_all | solution.py:35
  159.4 47.4 %all-to-all-start.4 = ((bf16[32,4,1792]{2,1,0:T(4,128)(2,1)}), bf16[32,4,1792]{2,1,0:T(4,128)(2,1)S(1)}, u32[]{:S(2)}, u32[]{:S(2)}) async-start(bf16[32,4,1792]{2,1,0:T(4,128)(2,1)} %reshape.230), calls=%async_computation.4 | async-start | bytes 917504 | tf_op jit(solution)/shard_map/all_to_all | solution.py:54
  172.9 27.4 %copy-start.4 = (bf16[128,1792]{1,0:T(8,128)(2,1)S(1)}, bf16[128,1792]{1,0:T(8,128)(2,1)}, u32[]{:S(2)}) copy-start(bf16[128,1792]{1,0:T(8,128)(2,1)} %convert_element_type.134) | copy-start | bytes 1376260
  172.9 35.8 %copy-start.1 = (bf16[8,7168]{1,0:T(8,128)(2,1)S(1)}, bf16[8,7168]{1,0:T(8,128)(2,1)}, u32[]{:S(2)}) copy-start(bf16[8,7168]{1,0:T(8,128)(2,1)} %param.9) | copy-start | bytes 344068
  200.3 5.6 %copy-start.5 = (s32[8,4]{0,1:T(4,128)S(1)}, s32[8,4]{0,1:T(4,128)}, u32[]{:S(2)}) copy-start(s32[8,4]{0,1:T(4,128)} %param.7) | copy-start | bytes 388
Sparse Core Ops, SparseCore 0:
  81.0 40.5 all-reduce.2
where the time goes:
time: 216 us
  waiting for transfers between devices  78.9 us (37%)
  matrix products  52.1 us (24%)
  local copies, waits for them, and re-layouts  38.7 us (18%)
  starting transfers between devices  25.6 us (12%)
  between operations  14.3 us (7%)
  other arithmetic  6.05 us (3%)
    psum x1, waiting for transfers between devices, reduce_parts(): lax.psum(partial_term.astype(jnp.bfloat16), 'erow').astype(jnp.float32)  39.5 us
    unnamed x18, local copies, waits for them, and re-layouts  27.5 us
    dot_general x1, matrix products, on_device(): jnp.einsum('rd,dgf->rgf', x_rows, w_in, preferred_element_type=jnp.float32)  15.3 us
    all_to_all x1, waiting for transfers between devices, send_rows(): lax.all_to_all(x_out, ('erow', 'ecol'), split_axis=0, concat_axis=0, tile...  13.7 us
    dot_general x1, matrix products, on_device(): jnp.einsum('rgf,dgf->rd', grad_pre, w_in, preferred_element_type=jnp.floa...  13.3 us
    all_to_all x1, waiting for transfers between devices, send_rows(): lax.all_to_all(cot_out, ('erow', 'ecol'), split_axis=0, concat_axis=0, ti...  12.9 us
    all_to_all x1, starting transfers between devices, send_rows(): lax.all_to_all(prob_out, ('erow', 'ecol'), split_axis=0, concat_axis=0, t...  7.3 us
    dot_general x1, matrix products, on_device(): jnp.einsum('rd,rgf->dgf', x_rows, grad_pre, preferred_element_type=jnp.fl...  7.29 us
  transfers between devices with their start and end apart: 7, of which 6 were waited for; matrix products, arithmetic and copies ran while one was open for 29% of the time, Pallas kernels for 0%

commit v1 on v0

v1 whole, which is shorter than its diff:
```python
import functools

import jax
import jax.numpy as jnp
from jax import lax
from jax.experimental import pallas as pl
from jax.experimental.pallas import tpu as pltpu
from jax.sharding import PartitionSpec as P

BF16 = jnp.bfloat16
F32 = jnp.float32
BOTH = ("erow", "ecol")
VMEM_LIMIT = 48 * 1024 * 1024


def dot(a, b, ca=1, cb=0):
    return lax.dot_general(a, b, (((ca,), (cb,)), ((), ())), preferred_element_type=F32)


def params():
    return pltpu.CompilerParams(vmem_limit_bytes=VMEM_LIMIT)


def cost(flops, bytes_accessed):
    return pl.CostEstimate(flops=int(flops), bytes_accessed=int(bytes_accessed), transcendentals=0)


def whole(shape):
    return pl.BlockSpec(shape, lambda *_: (0,) * len(shape))


def slots_kernel(experts, capacity, routes_ref, gate_ref, tok_ref, cot_ref, x_ref, sc_ref, place_ref, weight_ref):
    count, top = routes_ref.shape
    slots = experts * capacity
    width = x_ref.shape[2]
    slot = lax.broadcasted_iota(jnp.int32, (count, slots), 1)
    expert, rank = slot // capacity, slot % capacity
    member = jnp.zeros((count, slots), F32)
    prob = jnp.zeros((count, slots), F32)
    for k in range(top):
        hit = routes_ref[:, k : k + 1] == expert
        member = member + jnp.where(hit, 1.0, 0.0)
        prob = prob + jnp.where(hit, gate_ref[:, k : k + 1].astype(F32), 0.0)
    row = lax.broadcasted_iota(jnp.int32, (count, count), 0)
    col = lax.broadcasted_iota(jnp.int32, (count, count), 1)
    earlier = jnp.where(col < row, 1.0, 0.0)
    prior = dot(earlier, member)
    placed = (member > 0.5) & (prior == rank.astype(F32))
    place = jnp.where(placed, 1.0, 0.0).astype(BF16)
    weight = jnp.where(placed, prob, 0.0).astype(BF16)
    place_ref[...] = place
    weight_ref[...] = weight
    for r in range(x_ref.shape[0] // experts):
        span = slice(r * width, (r + 1) * width)
        rows = slice(r * experts, (r + 1) * experts)
        x_ref[rows] = dot(place, tok_ref[:, span], 0, 0).astype(BF16).reshape(experts, capacity, width)
        sc_ref[rows] = dot(weight, cot_ref[:, span], 0, 0).astype(BF16).reshape(experts, capacity, width)


def to_slots(routes, gate_probs, tokens, cotangent, n_row, experts, capacity):
    count, model = tokens.shape
    slots = experts * capacity
    sent = jax.ShapeDtypeStruct((n_row * experts, capacity, model // n_row), BF16)
    table = jax.ShapeDtypeStruct((count, slots), BF16)
    return pl.pallas_call(
        functools.partial(slots_kernel, experts, capacity),
        out_shape=(sent, sent, table, table),
        compiler_params=params(),
        cost_estimate=cost(4 * slots * count * model, 10 * slots * model),
    )(routes, gate_probs, tokens, cotangent)


def exchange(rows):
    return lax.all_to_all(rows, BOTH, split_axis=0, concat_axis=0, tiled=True)


def pre_first_kernel(core_ref, x_ref, w_ref, out_ref, spread_ref):
    @pl.when(pl.program_id(0) == 0)
    def _():
        rows, width = spread_ref.shape[0] // 2, spread_ref.shape[1] // 2
        d = lax.broadcasted_iota(jnp.int32, (128, 256), 0)
        lane = lax.broadcasted_iota(jnp.int32, (128, 256), 1)
        x = x_ref[...].reshape(rows, width)
        for g in range(2):
            spread = jnp.where(lane == 2 * d + g, 1.0, 0.0).astype(BF16)
            for j in range(width // 128):
                part = dot(x[:, j * 128 : (j + 1) * 128], spread).astype(BF16)
                spread_ref[g * rows : (g + 1) * rows, j * 256 : (j + 1) * 256] = part

    w = w_ref[...].reshape(spread_ref.shape[1], w_ref.shape[2])
    out_ref[...] = dot(spread_ref[...], w).astype(out_ref.dtype)


def pre_second_kernel(core_ref, spread_ref, w_ref, out_ref):
    w = w_ref[...].reshape(spread_ref.shape[1], w_ref.shape[2])
    out_ref[...] = dot(spread_ref[...], w).astype(out_ref.dtype)


def pre_halves(core, x_in, w_in, rows):
    width, _, hidden = w_in.shape
    half = hidden // 2
    block = 256
    steps = half // block
    work = cost(8 * rows * width * half, 2 * width * hidden + 4 * rows * width)
    send, spread = pl.pallas_call(
        pre_first_kernel,
        grid_spec=pltpu.PrefetchScalarGridSpec(
            num_scalar_prefetch=1,
            grid=(steps,),
            in_specs=[
                whole(x_in.shape),
                pl.BlockSpec((width, 2, block), lambda i, c: (0, 0, (1 - c[0]) * steps + i)),
            ],
            out_specs=[
                pl.BlockSpec((2 * rows, block), lambda i, c: (0, i)),
                whole((2 * rows, 2 * width)),
            ],
        ),
        out_shape=(
            jax.ShapeDtypeStruct((2 * rows, half), BF16),
            jax.ShapeDtypeStruct((2 * rows, 2 * width), BF16),
        ),
        compiler_params=params(),
        cost_estimate=work,
    )(core, x_in, w_in)
    keep = pl.pallas_call(
        pre_second_kernel,
        grid_spec=pltpu.PrefetchScalarGridSpec(
            num_scalar_prefetch=1,
            grid=(steps,),
            in_specs=[
                whole((2 * rows, 2 * width)),
                pl.BlockSpec((width, 2, block), lambda i, c: (0, 0, c[0] * steps + i)),
            ],
            out_specs=pl.BlockSpec((2 * rows, block), lambda i, c: (0, i)),
        ),
        out_shape=jax.ShapeDtypeStruct((2 * rows, half), F32),
        compiler_params=params(),
        cost_estimate=work,
    )(core, spread, w_in)
    return send, keep, spread


def down_t_kernel(core_ref, sc_ref, w_ref, send_ref, keep_ref):
    sc = sc_ref[...].reshape(send_ref.shape[0], w_ref.shape[1])
    out = dot(sc, w_ref[...], 1, 1)
    step = pl.program_id(0)
    steps = pl.num_programs(0) // 2

    @pl.when(step < steps)
    def _():
        send_ref[...] = out.astype(send_ref.dtype)

    @pl.when(step >= steps)
    def _():
        keep_ref[...] = out


def down_t_halves(core, sc_in, w_out, rows):
    hidden, width = w_out.shape
    half = hidden // 2
    block = 256
    steps = half // block

    def w_index(i, c):
        own = i // steps
        return ((1 - c[0]) * (1 - own) + c[0] * own) * steps + i % steps, 0

    return pl.pallas_call(
        down_t_kernel,
        grid_spec=pltpu.PrefetchScalarGridSpec(
            num_scalar_prefetch=1,
            grid=(2 * steps,),
            in_specs=[whole(sc_in.shape), pl.BlockSpec((block, width), w_index)],
            out_specs=[
                pl.BlockSpec((rows, block), lambda i, c: (0, jnp.minimum(i, steps - 1))),
                pl.BlockSpec((rows, block), lambda i, c: (0, jnp.maximum(i - steps, 0))),
            ],
        ),
        out_shape=(
            jax.ShapeDtypeStruct((rows, half), BF16),
            jax.ShapeDtypeStruct((rows, half), F32),
        ),
        compiler_params=params(),
        cost_estimate=cost(2 * rows * width * hidden, 2 * width * hidden),
    )(core, sc_in, w_out)


def swap_cores(value):
    n_row = lax.axis_size("erow")
    return lax.ppermute(value, "erow", [(i, i ^ 1) for i in range(n_row)])


def sum_parts(send, keep):
    n_row = lax.axis_size("erow")
    pairs = n_row // 2
    chip_sum = (keep + swap_cores(send).astype(F32)).astype(BF16)
    total = chip_sum.astype(F32)
    for k in range(1, pairs):
        perm = [(i, ((i // 2 + k) % pairs) * 2 + i % 2) for i in range(n_row)]
        total = total + lax.ppermute(chip_sum, "erow", perm).astype(F32)
    return total


def expert_out_kernel(core_ref, own_ref, other_ref, w_ref, out_ref):
    half = own_ref.shape[1]
    core = core_ref[0]
    own = w_ref[pl.ds(pl.multiple_of(core * half, half), half), :]
    other = w_ref[pl.ds(pl.multiple_of((1 - core) * half, half), half), :]
    out = dot(own_ref[...], own) + dot(other_ref[...], other)
    out_ref[...] = out.astype(BF16).reshape(out_ref.shape)


def expert_out(core, own, other, w_out, capacity):
    rows, half = own.shape
    hidden, width = w_out.shape
    block = width // 7
    return pl.pallas_call(
        expert_out_kernel,
        grid_spec=pltpu.PrefetchScalarGridSpec(
            num_scalar_prefetch=1,
            grid=(7,),
            in_specs=[
                whole((rows, half)),
                whole((rows, half)),
                pl.BlockSpec((hidden, block), lambda i, c: (0, i)),
            ],
            out_specs=pl.BlockSpec((rows // capacity, capacity, block), lambda i, c: (0, 0, i)),
        ),
        out_shape=jax.ShapeDtypeStruct((rows // capacity, capacity, width), BF16),
        compiler_params=params(),
        cost_estimate=cost(2 * rows * width * hidden, 2 * width * hidden),
    )(core, own, other, w_out)


def join_halves(core_ref, own_ref, other_ref, joined):
    half = own_ref.shape[1]
    core = core_ref[0]
    joined[:, pl.ds(pl.multiple_of(core * half, half), half)] = own_ref[...]
    joined[:, pl.ds(pl.multiple_of((1 - core) * half, half), half)] = other_ref[...]


def grad_rows_kernel(core_ref, own_ref, other_ref, w_ref, out_ref, joined, product):
    @pl.when(pl.program_id(0) == 0)
    def _():
        join_halves(core_ref, own_ref, other_ref, joined)

    block = w_ref.shape[0]
    rows = joined.shape[0] // 2
    w = w_ref[...].reshape(2 * block, joined.shape[1])
    out = dot(w, joined[...], 1, 1)
    chunks = rows // 128
    for j in range(2 * chunks):
        product[j] = out[:, j * 128 : (j + 1) * 128]
    capacity = out_ref.shape[1]
    for j in range(chunks):
        gate = product[j, pl.ds(0, block, stride=2), :]
        up = product[chunks + j, pl.ds(1, block, stride=2), :]
        turned = (gate + up).T.astype(BF16).reshape(128 // capacity, capacity, block)
        out_ref[j * 128 // capacity : (j + 1) * 128 // capacity] = turned


def grad_rows(core, own, other, w_in, capacity):
    rows = own.shape[0] // 2
    width, _, hidden = w_in.shape
    block = width // 7
    return pl.pallas_call(
        grad_rows_kernel,
        grid_spec=pltpu.PrefetchScalarGridSpec(
            num_scalar_prefetch=1,
            grid=(7,),
            in_specs=[
                whole(own.shape),
                whole(own.shape),
                pl.BlockSpec((block, 2, hidden), lambda i, c: (i, 0, 0)),
            ],
            out_specs=pl.BlockSpec((rows // capacity, capacity, block), lambda i, c: (0, 0, i)),
            scratch_shapes=[
                pltpu.VMEM((2 * rows, hidden), BF16),
                pltpu.VMEM((2 * rows // 128, 2 * block, 128), F32),
            ],
        ),
        out_shape=jax.ShapeDtypeStruct((rows // capacity, capacity, width), BF16),
        compiler_params=params(),
        cost_estimate=cost(8 * rows * width * hidden, 4 * width * hidden),
    )(core, own, other, w_in)


def grad_in_kernel(core_ref, own_ref, other_ref, spread_ref, out_ref, joined):
    @pl.when(pl.program_id(0) == 0)
    def _():
        join_halves(core_ref, own_ref, other_ref, joined)

    out = dot(spread_ref[...], joined[...], 0, 0)
    out_ref[...] = out.astype(BF16).reshape(out_ref.shape)


def grad_in(core, own, other, spread):
    both, half = own.shape
    hidden = 2 * half
    width = spread.shape[1] // 2
    block = 128
    return pl.pallas_call(
        grad_in_kernel,
        grid_spec=pltpu.PrefetchScalarGridSpec(
            num_scalar_prefetch=1,
            grid=(width // block,),
            in_specs=[
                whole(own.shape),
                whole(own.shape),
                pl.BlockSpec((both, 2 * block), lambda i, c: (0, i)),
            ],
            out_specs=pl.BlockSpec((block, 2, hidden), lambda i, c: (i, 0, 0)),
            scratch_shapes=[pltpu.VMEM((both, hidden), BF16)],
        ),
        out_shape=jax.ShapeDtypeStruct((width, 2, hidden), BF16),
        compiler_params=params(),
        cost_estimate=cost(4 * both * width * hidden, 4 * width * hidden),
    )(core, own, other, spread)


def grad_out_kernel(core_ref, own_ref, other_ref, sc_ref, out_ref):
    rows = own_ref.shape[0]
    sc = sc_ref[...].reshape(rows, out_ref.shape[1])
    step = pl.program_id(0)
    steps = pl.num_programs(0) // 2

    @pl.when(step < steps)
    def _():
        out_ref[...] = dot(own_ref[...], sc, 0, 0).astype(BF16)

    @pl.when(step >= steps)
    def _():
        out_ref[...] = dot(other_ref[...], sc, 0, 0).astype(BF16)


def grad_out(core, own, other, sc_in):
    rows, half = own.shape
    width = sc_in.shape[2]
    block = 256
    steps = half // block

    def out_index(i, c):
        second = i // steps
        return (c[0] * (1 - second) + (1 - c[0]) * second) * steps + i % steps, 0

    return pl.pallas_call(
        grad_out_kernel,
        grid_spec=pltpu.PrefetchScalarGridSpec(
            num_scalar_prefetch=1,
            grid=(2 * steps,),
            in_specs=[
                pl.BlockSpec((rows, block), lambda i, c: (0, jnp.minimum(i, steps - 1))),
                pl.BlockSpec((rows, block), lambda i, c: (0, jnp.maximum(i - steps, 0))),
                whole(sc_in.shape),
            ],
            out_specs=pl.BlockSpec((block, width), out_index),
        ),
        out_shape=jax.ShapeDtypeStruct((2 * half, width), BF16),
        compiler_params=params(),
        cost_estimate=cost(4 * rows * width * half, 4 * width * half),
    )(core, own, other, sc_in)


def layer_out_kernel(routes_ref, place_ref, weight_ref, cot_ref, rows_ref, out_ref, dprob_ref):
    count, slots = place_ref.shape
    _, capacity, width = rows_ref.shape
    experts = slots // capacity
    dots = jnp.zeros((count, slots), F32)
    for r in range(out_ref.shape[1] // width):
        span = slice(r * width, (r + 1) * width)
        part = rows_ref[r * experts : (r + 1) * experts].reshape(slots, width)
        out_ref[:, span] = dot(weight_ref[...], part).astype(BF16)
        dots = dots + dot(cot_ref[:, span], part, 1, 1)
    dots = jnp.where(place_ref[...].astype(F32) > 0.5, dots, 0.0)
    expert = lax.broadcasted_iota(jnp.int32, (count, slots), 1) // capacity
    column = lax.broadcasted_iota(jnp.int32, dprob_ref.shape, 1)
    grads = jnp.zeros(dprob_ref.shape, F32)
    for k in range(dprob_ref.shape[1]):
        term = jnp.sum(jnp.where(routes_ref[:, k : k + 1] == expert, dots, 0.0), axis=1, keepdims=True)
        grads = grads + jnp.where(column == k, term, 0.0)
    dprob_ref[...] = grads


def layer_out(routes, place, weight, cotangent, returned):
    return pl.pallas_call(
        layer_out_kernel,
        out_shape=(
            jax.ShapeDtypeStruct(cotangent.shape, BF16),
            jax.ShapeDtypeStruct(routes.shape, F32),
        ),
        compiler_params=params(),
        cost_estimate=cost(4 * returned.size * 8, 2 * returned.size),
    )(routes, place, weight, cotangent, returned)


def token_grads_kernel(place_ref, rows_ref, out_ref):
    slots = place_ref.shape[1]
    _, capacity, width = rows_ref.shape
    experts = slots // capacity
    for r in range(out_ref.shape[1] // width):
        part = rows_ref[r * experts : (r + 1) * experts].reshape(slots, width)
        out_ref[:, r * width : (r + 1) * width] = dot(place_ref[...], part).astype(BF16)


def token_grads(place, returned, model):
    return pl.pallas_call(
        token_grads_kernel,
        out_shape=jax.ShapeDtypeStruct((place.shape[0], model), BF16),
        compiler_params=params(),
        cost_estimate=cost(2 * returned.size * 8, 2 * returned.size),
    )(place, returned)


def on_device(tokens, routes, gate_probs, cotangent, w_gate_up, w_down):
    n_row = lax.axis_size("erow")
    experts = lax.axis_size("ecol")
    count, model = tokens.shape
    capacity = count // 2
    rows = n_row * experts * capacity
    core = (lax.axis_index("erow") % 2).astype(jnp.int32).reshape(1)
    w_in = w_gate_up[0]
    w_out = w_down[0]

    x_out, sc_out, place, weight = to_slots(
        routes, gate_probs, tokens, cotangent, n_row, experts, capacity
    )
    x_in = exchange(x_out)
    sc_in = exchange(sc_out)

    pre_send, pre_keep, spread = pre_halves(core, x_in, w_in, rows)
    pre = sum_parts(pre_send, pre_keep)
    gate, up = pre[:rows], pre[rows:]
    s = jax.nn.sigmoid(gate)
    activated = gate * s
    hidden_own = (activated * up).astype(BF16)
    hidden_other = swap_cores(hidden_own)
    out_rows = expert_out(core, hidden_own, hidden_other, w_out, capacity)
    out_back = exchange(out_rows)

    hid_send, hid_keep = down_t_halves(core, sc_in, w_out, rows)
    grad_hidden = sum_parts(hid_send, hid_keep)
    grad_gate = grad_hidden * up * s * (1.0 + gate * (1.0 - s))
    grad_up = grad_hidden * activated
    grad_own = jnp.concatenate([grad_gate, grad_up], axis=0).astype(BF16)
    grad_other = swap_cores(grad_own)
    back_rows = grad_rows(core, grad_own, grad_other, w_in, capacity)
    grad_back = exchange(back_rows)

    grad_down = grad_out(core, hidden_own, hidden_other, sc_in)[None]
    grad_gate_up = grad_in(core, grad_own, grad_other, spread)[None]
    out, grad_probs = layer_out(routes, place, weight, cotangent, out_back)
    grad_tokens = token_grads(place, grad_back, model)
    return (out, grad_tokens, grad_probs, grad_gate_up, grad_down)


def solution(mesh):
    flat = P(BOTH, None)
    return jax.shard_map(
        on_device,
        mesh=mesh,
        in_specs=(flat, flat, flat, flat, P("ecol", "erow", None, None), P("ecol", None, "erow")),
        out_specs=(flat, flat, flat, P("ecol", "erow", None, None), P("ecol", None, "erow")),
        check_vma=False,
    )
```

time: 216 us -> 122 us (0.56)
  Pallas kernels: 0 us -> 57.9 us
  matrix products: 52.1 us -> 0 us
  waiting for transfers between devices: 78.9 us -> 28.4 us
  local copies, waits for them, and re-layouts: 38.7 us -> 7.2 us
  between operations: 14.3 us -> 0.78 us
  other arithmetic: 6.05 us -> 2.58 us
    pallas_call x0 -> x10, Pallas kernels: none -> 57.9 us  [the longest x1 10.8 us: grad_in(): pl.pallas_call(grad_in_kernel, grid_spec=pltpu.PrefetchScalarGridSpec(num...]
    dot_general x10 -> x0, matrix products: 52.1 us -> none  [the longest x1 15.3 us: on_device(): jnp.einsum('rd,dgf->rgf', x_rows, w_in, preferred_element_type=jnp.float32)]
    psum x1 -> x0, waiting for transfers between devices: 39.5 us -> none  [reduce_parts(): lax.psum(partial_term.astype(jnp.bfloat16), 'erow').astype(jnp.float32)]
    all_to_all x6 -> x4, waiting for transfers between devices: 39.4 us -> 16 us  [exchange(): return lax.all_to_all(rows, BOTH, split_axis=0, concat_axis=0, tiled=True)]
    unnamed x18 -> x19, local copies, waits for them, and re-layouts: 27.5 us -> 7.2 us
    ppermute x0 -> x6, waiting for transfers between devices: none -> 12.3 us  [the longest x2 7.62 us: sum_parts(): total = total + lax.ppermute(chip_sum, 'erow', perm).astype(F32)]
    reshape x9 -> x0, local copies, waits for them, and re-layouts: 6.98 us -> none  [the longest x2 3.16 us: send_rows(): x_in.reshape(-1, weight_slice)]
    all_to_all x6 -> x4, starting transfers between devices: 25.6 us -> 21.2 us  [exchange(): return lax.all_to_all(rows, BOTH, split_axis=0, concat_axis=0, tiled=True)]
  transfers between devices with their start and end apart: 7 -> 10, of which waited for: 6 -> 8; matrix products, arithmetic and copies ran while one was open for 29% -> 2% of each run, Pallas kernels for 0% -> 39%
where the time goes in v1:
time: 122 us; the launch traced here: 121 us
  Pallas kernels  57.9 us (47%)
  waiting for transfers between devices  28.4 us (23%)
  starting transfers between devices  24.1 us (20%)
  local copies, waits for them, and re-layouts  7.2 us (6%)
  other arithmetic  2.58 us (2%)
    all_to_all x4, starting transfers between devices, exchange(): return lax.all_to_all(rows, BOTH, split_axis=0, concat_axis=0, tiled=True)  21.2 us
    all_to_all x4, waiting for transfers between devices, exchange(): return lax.all_to_all(rows, BOTH, split_axis=0, concat_axis=0, tiled=True)  16 us
    pallas_call x1, Pallas kernels, grad_in(): pl.pallas_call(grad_in_kernel, grid_spec=pltpu.PrefetchScalarGridSpec(num...  10.8 us
    pallas_call x1, Pallas kernels, grad_rows(): pl.pallas_call(grad_rows_kernel, grid_spec=pltpu.PrefetchScalarGridSpec(n...  10.1 us
    ppermute x2, waiting for transfers between devices, sum_parts(): total = total + lax.ppermute(chip_sum, 'erow', perm).astype(F32)  7.62 us
    pallas_call x1, Pallas kernels, down_t_halves(): pl.pallas_call(down_t_kernel, grid_spec=pltpu.PrefetchScalarGridSpec(num_...  7.49 us
    unnamed x19, local copies, waits for them, and re-layouts  7.2 us
    pallas_call x1, Pallas kernels, expert_out(): pl.pallas_call(expert_out_kernel, grid_spec=pltpu.PrefetchScalarGridSpec(...  7.07 us
  transfers between devices with their start and end apart: 10, of which 8 were waited for; matrix products, arithmetic and copies ran while one was open for 2% of the time, Pallas kernels for 39%

profile of v1, /device:TPU:0, one launch (start us, length us, event | category | flops | bytes accessed | tf_op | source)
XLA Modules:
  0.0 120.9 jit_solution(16964522174625793562)
XLA Ops:
  0.6 0.8 copy.13.routes_ref
  1.4 0.8 copy.12.gate_ref
  2.2 0.9 copy-done.5
  3.1 0.9 copy-done.7
  4.0 1.5 %shard_map.101 = (bf16[32,4,1792]{2,1,0:T(4,128)(2,1)}, bf16[32,4,1792]{2,1,0:T(4,128)(2,1)}, bf16[8,32]{1,0:T(8,128)(2,1)S(1)}, bf16[8,32]{1,0:T(8,128)(2,1)S(1)}) custom-call(s32[8,4]{1,0:T(8,128)S(1)} %copy.13.routes_ref, bf16[8,4]{1,0:T(8,128)(2,1)S(1)} %copy.12.gate_ref, bf16[8,7168]{1,0:T(8,128)(2,1)S(1)} %copy-done.7, bf16[8,7168]{1,0:T(8,128)(2,1)S(1)} %copy-done.5), custom_call_target="tpu_custom_call" | custom-call | flops 7340032 | bytes 2293760 | tf_op jit(solution)/shard_map/pallas_call | solution.py:65
  5.5 7.3 %all-to-all-start = ((bf16[32,4,1792]{2,1,0:T(4,128)(2,1)}), bf16[32,4,1792]{2,1,0:T(4,128)(2,1)S(1)}, u32[]{:S(2)}, u32[]{:S(2)}) async-start(bf16[32,4,1792]{2,1,0:T(4,128)(2,1)} %get-tuple-element.17), calls=%async_computation | async-start | bytes 917504 | tf_op jit(solution)/shard_map/all_to_all | solution.py:74
  12.8 14.9 %all-to-all-done.x_ref = bf16[32,4,1792]{2,1,0:T(4,128)(2,1)S(1)} async-done(((bf16[32,4,1792]{2,1,0:T(4,128)(2,1)}), bf16[32,4,1792]{2,1,0:T(4,128)(2,1)S(1)}, u32[]{:S(2)}, u32[]{:S(2)}) %all-to-all-start) | async-done | bytes 458784 | tf_op jit(solution)/shard_map/all_to_all | solution.py:74
  27.7 2.6 %all-to-all-start.2 = ((bf16[32,4,1792]{2,1,0:T(4,128)(2,1)}), bf16[32,4,1792]{2,1,0:T(4,128)(2,1)S(1)}, u32[]{:S(2)}, u32[]{:S(2)}) async-start(bf16[32,4,1792]{2,1,0:T(4,128)(2,1)} %get-tuple-element.21), calls=%async_computation.2 | async-start | bytes 917504 | tf_op jit(solution)/shard_map/all_to_all | solution.py:74
  30.3 6.3 %shard_map.102 = (bf16[256,1024]{1,0:T(8,128)(2,1)S(1)}, bf16[256,3584]{1,0:T(8,128)(2,1)S(1)}) custom-call(s32[1]{0:T(128)} %bitcast.core_ref, bf16[32,4,1792]{2,1,0:T(4,128)(2,1)S(1)} %all-to-all-done.x_ref, bf16[1792,2,2048]{2,1,0:T(2,128)(2,1)} %bitcast.5), custom_call_target="tpu_custom_call" | custom-call | flops 1879048192 | bytes 8257536 | tf_op jit(solution)/shard_map/pallas_call | solution.py:105
  36.8 5.7 %shard_map.103 = f32[256,1024]{1,0:T(8,128)S(1)} custom-call(s32[1]{0:T(128)} %bitcast.core_ref, bf16[256,3584]{1,0:T(8,128)(2,1)S(1)} %get-tuple-element.18.spread_ref, bf16[1792,2,2048]{2,1,0:T(2,128)(2,1)} %bitcast.6), custom_call_target="tpu_custom_call" | custom-call | flops 1879048192 | bytes 8257536 | tf_op jit(solution)/shard_map/pallas_call | solution.py:126
  42.7 1.7 %collective-permute-start.1 = (bf16[256,1024]{1,0:T(8,128)(2,1)S(1)}, bf16[256,1024]{1,0:T(8,128)(2,1)S(1)}, u32[]{:S(2)}, u32[]{:S(2)}) collective-permute-start(bf16[256,1024]{1,0:T(8,128)(2,1)S(1)} %add_convert_fusion), channel_id=1, source_target_pairs={{0,16},{8,24},{16,0},{24,8},{1,17},{9,25},{17,1},{25,9},{2,18},{10... | collective-permute-start | bytes 1572872 | tf_op jit(solution)/shard_map/ppermute | solution.py:201
  44.4 0.9 all-to-all-done.2.sc_ref
  45.3 7.5 %shard_map.106 = (bf16[128,1024]{1,0:T(8,128)(2,1)S(1)}, f32[128,1024]{1,0:T(8,128)S(1)}) custom-call(s32[1]{0:T(128)} %bitcast.core_ref, bf16[32,4,1792]{2,1,0:T(4,128)(2,1)S(1)} %all-to-all-done.2.sc_ref, bf16[2048,1792]{1,0:T(8,128)(2,1)} %bitcast.8), custom_call_target="tpu_custom_call" | custom-call | flops 939524096 | bytes 7340032 | tf_op jit(solution)/shard_map/pallas_call | solution.py:169
  52.8 1.5 %collective-permute-done.3 = bf16[128,1024]{1,0:T(8,128)(2,1)S(1)} collective-permute-done((bf16[128,1024]{1,0:T(8,128)(2,1)S(1)}, bf16[128,1024]{1,0:T(8,128)(2,1)S(1)}, u32[]{:S(2)}, u32[]{:S(2)}) %collective-permute-start.3) | collective-permute-done | bytes 262176 | tf_op jit(solution)/shard_map/ppermute | solution.py:191
  55.0 1.9 %collective-permute-done.1 = bf16[256,1024]{1,0:T(8,128)(2,1)S(1)} collective-permute-done((bf16[256,1024]{1,0:T(8,128)(2,1)S(1)}, bf16[256,1024]{1,0:T(8,128)(2,1)S(1)}, u32[]{:S(2)}, u32[]{:S(2)}) %collective-permute-start.1) | collective-permute-done | bytes 524320 | tf_op jit(solution)/shard_map/ppermute | solution.py:201
  57.2 5.7 %collective-permute-done.4 = bf16[128,1024]{1,0:T(8,128)(2,1)S(1)} collective-permute-done((bf16[128,1024]{1,0:T(8,128)(2,1)S(1)}, bf16[128,1024]{1,0:T(8,128)(2,1)S(1)}, u32[]{:S(2)}, u32[]{:S(2)}) %collective-permute-start.4) | collective-permute-done | bytes 262176 | tf_op jit(solution)/shard_map/ppermute | solution.py:201
  62.8 1.1 multiply_convert_fusion.1
  64.0 1.5 %collective-permute-done.2.other_ref = bf16[128,1024]{1,0:T(8,128)(2,1)S(1)} collective-permute-done((bf16[128,1024]{1,0:T(8,128)(2,1)S(1)}, bf16[128,1024]{1,0:T(8,128)(2,1)S(1)}, u32[]{:S(2)}, u32[]{:S(2)}) %collective-permute-start.2) | collective-permute-done | bytes 262176 | tf_op jit(solution)/shard_map/ppermute | solution.py:191
  65.5 7.1 %shard_map.104 = bf16[32,4,1792]{2,1,0:T(4,128)(2,1)} custom-call(s32[1]{0:T(128)} %bitcast.core_ref, bf16[128,1024]{1,0:T(8,128)(2,1)S(1)} %get-tuple-element.32.own_ref, bf16[128,1024]{1,0:T(8,128)(2,1)S(1)} %collective-permute-done.2.other_ref, bf16[2048,1792]{1,0:T(8,128)(2,1)} %bitcast.9), custom_call_target="tpu_custom_call" | custom-call | flops 939524096 | bytes 7340032 | tf_op jit(solution)/shard_map/pallas_call | solution.py:218
  72.6 0.7 copy-done.3
  73.3 5.6 %all-to-all-start.1 = ((bf16[32,4,1792]{2,1,0:T(4,128)(2,1)}), bf16[32,4,1792]{2,1,0:T(4,128)(2,1)S(1)}, u32[]{:S(2)}, u32[]{:S(2)}) async-start(bf16[32,4,1792]{2,1,0:T(4,128)(2,1)} %shard_map.104), calls=%async_computation.1 | async-start | bytes 917504 | tf_op jit(solution)/shard_map/all_to_all | solution.py:74
  78.8 1.1 pad_maximum_fusion.own_ref
  80.2 1.7 %collective-permute-done.5.other_ref = bf16[256,1024]{1,0:T(8,128)(2,1)S(1)} collective-permute-done((bf16[256,1024]{1,0:T(8,128)(2,1)S(1)}, bf16[256,1024]{1,0:T(8,128)(2,1)S(1)}, u32[]{:S(2)}, u32[]{:S(2)}) %collective-permute-start.5) | collective-permute-done | bytes 524320 | tf_op jit(solution)/shard_map/ppermute | solution.py:191
  81.9 10.1 %shard_map.107 = bf16[32,4,1792]{2,1,0:T(4,128)(2,1)S(1)} custom-call(s32[1]{0:T(128)} %bitcast.core_ref, bf16[256,1024]{1,0:T(8,128)(2,1)S(1)} %pad_maximum_fusion.own_ref, bf16[256,1024]{1,0:T(8,128)(2,1)S(1)} %collective-permute-done.5.other_ref, bf16[1792,2,2048]{2,1,0:T(2,128)(2,1)} %bitcast.7), custom_call_target="tpu_custom_call" | custom-call | flops 3758096384 | bytes 14680064 | tf_op jit(solution)/shard_map/pallas_call | solution.py:267
  92.0 0.8 copy-done
  92.8 0.8 copy-done.2
  93.8 5.7 %all-to-all-start.3 = ((bf16[32,4,1792]{2,1,0:T(4,128)(2,1)}), bf16[32,4,1792]{2,1,0:T(4,128)(2,1)}, u32[]{:S(2)}, u32[]{:S(2)}) async-start(bf16[32,4,1792]{2,1,0:T(4,128)(2,1)} %copy-done.2), calls=%async_computation.3 | async-start | bytes 917504 | tf_op jit(solution)/shard_map/all_to_all | solution.py:74
  99.5 0.9 copy-done.4
  100.5 6.2 %shard_map.110 = bf16[2048,1792]{1,0:T(8,128)(2,1)} custom-call(s32[1]{0:T(128)} %bitcast.core_ref, bf16[128,1024]{1,0:T(8,128)(2,1)S(1)} %get-tuple-element.32.own_ref, bf16[128,1024]{1,0:T(8,128)(2,1)S(1)} %copy-done.4, bf16[32,4,1792]{2,1,0:T(4,128)(2,1)S(1)} %all-to-all-done.2.sc_ref), custom_call_target="tpu_custom_call" | custom-call | flops 939524096 | bytes 7340032 | tf_op jit(solution)/shard_map/pallas_call | solution.py:347
  106.7 10.8 %shard_map.109 = bf16[1792,2,2048]{2,1,0:T(2,128)(2,1)} custom-call(s32[1]{0:T(128)} %bitcast.core_ref, bf16[256,1024]{1,0:T(8,128)(2,1)S(1)} %pad_maximum_fusion.own_ref, bf16[256,1024]{1,0:T(8,128)(2,1)S(1)} %copy-done.1, bf16[256,3584]{1,0:T(8,128)(2,1)S(1)} %get-tuple-element.18.spread_ref), custom_call_target="tpu_custom_call" | custom-call | flops 3758096384 | bytes 14680064 | tf_op jit(solution)/shard_map/pallas_call | solution.py:303
  117.5 1.0 shard_map.105
  119.1 1.9 %shard_map.108 = bf16[8,7168]{1,0:T(8,128)(2,1)} custom-call(bf16[8,32]{1,0:T(8,128)(2,1)S(1)} %get-tuple-element.15.place_ref, bf16[32,4,1792]{2,1,0:T(4,128)(2,1)} %all-to-all-done.3.rows_ref), custom_call_target="tpu_custom_call" | custom-call | flops 3670016 | bytes 458752 | tf_op jit(solution)/shard_map/pallas_call | solution.py:407
  (22 shorter events, 2.5 us)
Async XLA Ops:
  2.2 0.9 copy-start.5
  3.1 0.9 copy-start.7
  5.5 22.3 %all-to-all-start = ((bf16[32,4,1792]{2,1,0:T(4,128)(2,1)}), bf16[32,4,1792]{2,1,0:T(4,128)(2,1)S(1)}, u32[]{:S(2)}, u32[]{:S(2)}) async-start(bf16[32,4,1792]{2,1,0:T(4,128)(2,1)} %get-tuple-element.17), calls=%async_computation | async-start | bytes 917504 | tf_op jit(solution)/shard_map/all_to_all | solution.py:74
  27.7 17.6 %all-to-all-start.2 = ((bf16[32,4,1792]{2,1,0:T(4,128)(2,1)}), bf16[32,4,1792]{2,1,0:T(4,128)(2,1)S(1)}, u32[]{:S(2)}, u32[]{:S(2)}) async-start(bf16[32,4,1792]{2,1,0:T(4,128)(2,1)} %get-tuple-element.21), calls=%async_computation.2 | async-start | bytes 917504 | tf_op jit(solution)/shard_map/all_to_all | solution.py:74
  36.6 5.8 %collective-permute-start = (bf16[256,1024]{1,0:T(8,128)(2,1)S(1)}, bf16[256,1024]{1,0:T(8,128)(2,1)S(1)}, u32[]{:S(2)}, u32[]{:S(2)}) collective-permute-start(bf16[256,1024]{1,0:T(8,128)(2,1)S(1)} %get-tuple-element.19), channel_id=1, source_target_pairs={{0,8},{8,0},{16,24},{24,16},{1,9},{9,1},{17,25},{25,17},{2,10},{10... | collective-permute-start | bytes 1572872 | tf_op jit(solution)/shard_map/ppermute | solution.py:191
  42.7 14.3 %collective-permute-start.1 = (bf16[256,1024]{1,0:T(8,128)(2,1)S(1)}, bf16[256,1024]{1,0:T(8,128)(2,1)S(1)}, u32[]{:S(2)}, u32[]{:S(2)}) collective-permute-start(bf16[256,1024]{1,0:T(8,128)(2,1)S(1)} %add_convert_fusion), channel_id=1, source_target_pairs={{0,16},{8,24},{16,0},{24,8},{1,17},{9,25},{17,1},{25,9},{2,18},{10... | collective-permute-start | bytes 1572872 | tf_op jit(solution)/shard_map/ppermute | solution.py:201
  52.8 1.6 %collective-permute-start.3 = (bf16[128,1024]{1,0:T(8,128)(2,1)S(1)}, bf16[128,1024]{1,0:T(8,128)(2,1)S(1)}, u32[]{:S(2)}, u32[]{:S(2)}) collective-permute-start(bf16[128,1024]{1,0:T(8,128)(2,1)S(1)} %get-tuple-element.23), channel_id=1, source_target_pairs={{0,8},{8,0},{16,24},{24,16},{1,9},{9,1},{17,25},{25,17},{2,10},{10... | collective-permute-start | bytes 786440 | tf_op jit(solution)/shard_map/ppermute | solution.py:191
  54.4 8.4 %collective-permute-start.4 = (bf16[128,1024]{1,0:T(8,128)(2,1)S(1)}, bf16[128,1024]{1,0:T(8,128)(2,1)S(1)}, u32[]{:S(2)}, u32[]{:S(2)}) collective-permute-start(bf16[128,1024]{1,0:T(8,128)(2,1)S(1)} %add_convert_fusion.1), channel_id=1, source_target_pairs={{0,16},{8,24},{16,0},{24,8},{1,17},{9,25},{17,1},{25,9},{2,18},{10... | collective-permute-start | bytes 786440 | tf_op jit(solution)/shard_map/ppermute | solution.py:201
  64.0 1.5 %collective-permute-start.2 = (bf16[128,1024]{1,0:T(8,128)(2,1)S(1)}, bf16[128,1024]{1,0:T(8,128)(2,1)S(1)}, u32[]{:S(2)}, u32[]{:S(2)}) collective-permute-start(bf16[128,1024]{1,0:T(8,128)(2,1)S(1)} %get-tuple-element.32.own_ref), channel_id=1, source_target_pairs={{0,8},{8,0},{16,24},{24,16},{1,9},{9,1},{17,25},{25,17},{2,10},{10... | collective-permute-start | bytes 786440 | tf_op jit(solution)/shard_map/ppermute | solution.py:191
  72.6 0.7 copy-start.3
  73.3 20.5 %all-to-all-start.1 = ((bf16[32,4,1792]{2,1,0:T(4,128)(2,1)}), bf16[32,4,1792]{2,1,0:T(4,128)(2,1)S(1)}, u32[]{:S(2)}, u32[]{:S(2)}) async-start(bf16[32,4,1792]{2,1,0:T(4,128)(2,1)} %shard_map.104), calls=%async_computation.1 | async-start | bytes 917504 | tf_op jit(solution)/shard_map/all_to_all | solution.py:74
  79.9 2.0 %collective-permute-start.5 = (bf16[256,1024]{1,0:T(8,128)(2,1)S(1)}, bf16[256,1024]{1,0:T(8,128)(2,1)S(1)}, u32[]{:S(2)}, u32[]{:S(2)}) collective-permute-start(bf16[256,1024]{1,0:T(8,128)(2,1)S(1)} %pad_maximum_fusion.own_ref), channel_id=1, source_target_pairs={{0,8},{8,0},{16,24},{24,16},{1,9},{9,1},{17,25},{25,17},{2,10},{10... | collective-permute-start | bytes 1572872 | tf_op jit(solution)/shard_map/ppermute | solution.py:191
  92.0 0.8 copy-start
  92.8 0.8 copy-start.2
  93.8 25.3 %all-to-all-start.3 = ((bf16[32,4,1792]{2,1,0:T(4,128)(2,1)}), bf16[32,4,1792]{2,1,0:T(4,128)(2,1)}, u32[]{:S(2)}, u32[]{:S(2)}) async-start(bf16[32,4,1792]{2,1,0:T(4,128)(2,1)} %copy-done.2), calls=%async_computation.3 | async-start | bytes 917504 | tf_op jit(solution)/shard_map/all_to_all | solution.py:74
  99.5 1.0 copy-start.4
  100.5 6.2 %copy-start.1 = (bf16[256,1024]{1,0:T(8,128)(2,1)S(1)}, bf16[256,1024]{1,0:T(8,128)(2,1)}, u32[]{:S(2)}) copy-start(bf16[256,1024]{1,0:T(8,128)(2,1)} %copy-done) | copy-start | bytes 1572868
  106.7 10.8 %copy-start.6 = (bf16[8,7168]{1,0:T(8,128)(2,1)S(1)}, bf16[8,7168]{1,0:T(8,128)(2,1)}, u32[]{:S(2)}) copy-start(bf16[8,7168]{1,0:T(8,128)(2,1)} %cot_ref.3) | copy-start | bytes 344068

commit v2 on v0

v2 whole, which is shorter than its diff:
```python
import functools

import jax
import jax.numpy as jnp
from jax import lax
from jax.experimental import pallas as pl
from jax.experimental.pallas import tpu as pltpu
from jax.sharding import PartitionSpec as P

BF16 = jnp.bfloat16
F32 = jnp.float32
BOTH = ("erow", "ecol")
MIB = 1024 * 1024
HBM = pl.BlockSpec(memory_space=pltpu.HBM)
VMEM = pl.BlockSpec(memory_space=pltpu.VMEM)
SMEM = pl.BlockSpec(memory_space=pltpu.SMEM)


def dot(a, b, ca=1, cb=0):
    return lax.dot_general(a, b, (((ca,), (cb,)), ((), ())), preferred_element_type=F32)


def params(mib):
    return pltpu.CompilerParams(vmem_limit_bytes=mib * MIB)


def cost(flops, bytes_accessed):
    return pl.CostEstimate(flops=int(flops), bytes_accessed=int(bytes_accessed), transcendentals=0)


def in_hbm(array):
    return pltpu.with_memory_space_constraint(array, pltpu.HBM)


def shape(*dims, dtype=BF16):
    return jax.ShapeDtypeStruct(dims, dtype)


def aligned(value, step):
    return pl.multiple_of(value * step, step)


def slot_tables(routes_ref, gate_ref, experts, capacity, group=1):
    top, count = routes_ref.shape
    dims = (experts * group * capacity, count)
    slot = lax.broadcasted_iota(jnp.int32, dims, 0)
    expert, rank = slot // (group * capacity), slot % capacity
    member = jnp.zeros(dims, F32)
    prob = jnp.zeros(dims, F32)
    for k in range(top):
        hit = routes_ref[k : k + 1, :] == expert
        member = member + jnp.where(hit, 1.0, 0.0)
        prob = prob + jnp.where(hit, gate_ref[k : k + 1, :].astype(F32), 0.0)
    before = lax.broadcasted_iota(jnp.int32, (count, count), 0)
    after = lax.broadcasted_iota(jnp.int32, (count, count), 1)
    prior = dot(member, jnp.where(before < after, 1.0, 0.0))
    placed = (member > 0.5) & (prior == rank.astype(F32))
    return placed, prob


def slots_kernel(experts, capacity, weighted, routes_hbm, gate_hbm, rows_hbm, out_ref, routes_ref, gate_ref, rows, sems):
    loads = [
        pltpu.make_async_copy(source, target, sems.at[i])
        for i, (source, target) in enumerate(
            ((routes_hbm, routes_ref), (gate_hbm, gate_ref), (rows_hbm, rows))
        )
    ]
    for load in loads:
        load.start()
    loads[0].wait()
    loads[1].wait()
    placed, prob = slot_tables(routes_ref, gate_ref, experts, capacity)
    table = jnp.where(placed, prob if weighted else 1.0, 0.0).astype(BF16)
    loads[2].wait()
    width = out_ref.shape[2]
    for r in range(out_ref.shape[0] // experts):
        part = dot(table, rows[:, r * width : (r + 1) * width]).astype(BF16)
        out_ref[r * experts : (r + 1) * experts] = part.reshape(experts, capacity, width)


def to_slots(routes, gate_probs, rows, weighted, n_row, experts, capacity):
    count, model = rows.shape
    return pl.pallas_call(
        functools.partial(slots_kernel, experts, capacity, weighted),
        in_specs=[HBM, HBM, HBM],
        out_shape=shape(n_row * experts, capacity, model // n_row),
        scratch_shapes=[
            pltpu.VMEM(routes.shape, routes.dtype),
            pltpu.VMEM(gate_probs.shape, BF16),
            pltpu.VMEM(rows.shape, BF16),
            pltpu.SemaphoreType.DMA((3,)),
        ],
        compiler_params=params(8),
        cost_estimate=cost(2 * experts * capacity * count * model, 2 * rows.size),
    )(in_hbm(routes), in_hbm(gate_probs), in_hbm(rows))


def exchange(rows):
    return lax.all_to_all(rows, BOTH, split_axis=0, concat_axis=0, tiled=True)


def stream(copies, ahead=2):
    for copy in copies[:ahead]:
        copy.start()

    def block(i):
        copies[i].wait()
        if i + ahead < len(copies):
            copies[i + ahead].start()

    return block


def spread_rows(x, spread_ref):
    rows, width = x.shape
    d = lax.broadcasted_iota(jnp.int32, (128, 256), 0)
    lane = lax.broadcasted_iota(jnp.int32, (128, 256), 1)
    for g in range(2):
        pattern = jnp.where(lane == 2 * d + g, 1.0, 0.0).astype(BF16)
        for j in range(width // 128):
            part = dot(x[:, j * 128 : (j + 1) * 128], pattern).astype(BF16)
            spread_ref[g * rows : (g + 1) * rows, j * 256 : (j + 1) * 256] = part


def pre_kernel(core_ref, x_ref, w_hbm, send_ref, keep_ref, spread_ref, buffer, sems):
    steps, width, _, block = buffer.shape
    each = steps // 2

    def copy(i):
        part = 1 - core_ref[0] if i < each else core_ref[0]
        source = w_hbm.at[:, :, pl.ds(aligned(part * each + i % each, block), block)]
        return pltpu.make_async_copy(source, buffer.at[i], sems.at[i])

    ready = stream([copy(i) for i in range(steps)])
    spread_rows(x_ref[...].reshape(spread_ref.shape[0] // 2, width), spread_ref)
    for i in range(steps):
        ready(i)
        out_ref = send_ref if i < each else keep_ref
        out = dot(spread_ref[...], buffer[i].reshape(2 * width, block))
        out_ref[:, i % each * block : (i % each + 1) * block] = out.astype(out_ref.dtype)


def pre_halves(core, x_in, w_in, rows):
    width, _, hidden = w_in.shape
    half = hidden // 2
    steps = 4
    return pl.pallas_call(
        pre_kernel,
        in_specs=[SMEM, VMEM, HBM],
        out_specs=[VMEM, VMEM, VMEM],
        out_shape=(
            shape(2 * rows, half),
            shape(2 * rows, half, dtype=F32),
            shape(2 * rows, 2 * width),
        ),
        scratch_shapes=[
            pltpu.VMEM((steps, width, 2, hidden // steps), BF16),
            pltpu.SemaphoreType.DMA((steps,)),
        ],
        compiler_params=params(28),
        cost_estimate=cost(1e10, 4 * width * hidden),
    )(core, x_in, in_hbm(w_in))


def down_t_kernel(core_ref, sc_ref, w_hbm, send_ref, keep_ref, buffer, sems):
    steps, block, width = buffer.shape
    each = steps // 2

    def copy(i):
        part = 1 - core_ref[0] if i < each else core_ref[0]
        source = w_hbm.at[pl.ds(aligned(part * each + i % each, block), block), :]
        return pltpu.make_async_copy(source, buffer.at[i], sems.at[i])

    ready = stream([copy(i) for i in range(steps)])
    sc = sc_ref[...].reshape(send_ref.shape[0], width)
    for i in range(steps):
        ready(i)
        out_ref = send_ref if i < each else keep_ref
        out = dot(sc, buffer[i], 1, 1)
        out_ref[:, i % each * block : (i % each + 1) * block] = out.astype(out_ref.dtype)


def down_t_halves(core, sc_in, w_out, rows):
    hidden, width = w_out.shape
    half = hidden // 2
    steps = 4
    return pl.pallas_call(
        down_t_kernel,
        in_specs=[SMEM, VMEM, HBM],
        out_specs=[VMEM, VMEM],
        out_shape=(shape(rows, half), shape(rows, half, dtype=F32)),
        scratch_shapes=[
            pltpu.VMEM((steps, hidden // steps, width), BF16),
            pltpu.SemaphoreType.DMA((steps,)),
        ],
        compiler_params=params(16),
        cost_estimate=cost(2 * rows * width * hidden, 2 * width * hidden),
    )(core, sc_in, in_hbm(w_out))


def swap_cores(value):
    n_row = lax.axis_size("erow")
    return lax.ppermute(value, "erow", [(i, i ^ 1) for i in range(n_row)])


def sum_parts(send, keep):
    n_row = lax.axis_size("erow")
    pairs = n_row // 2
    chip_sum = (keep + swap_cores(send).astype(F32)).astype(BF16)
    others = []
    for k in range(1, pairs):
        perm = [(i, ((i // 2 + k) % pairs) * 2 + i % 2) for i in range(n_row)]
        others.append(lax.ppermute(chip_sum, "erow", perm))
    return chip_sum, others


def total(part, others):
    out = part.astype(F32)
    for other in others:
        out = out + other.astype(F32)
    return out


def expert_out_kernel(spans, core_ref, own_ref, other_ref, w_hbm, out_ref, joined, buffer, sems):
    copies = [
        pltpu.make_async_copy(w_hbm.at[:, pl.ds(at, size)], buffer.at[:, pl.ds(at, size)], sems.at[i])
        for i, (at, size) in enumerate(spans)
    ]
    ready = stream(copies)
    join_halves(core_ref, own_ref, other_ref, joined)
    for i, (at, size) in enumerate(spans):
        ready(i)
        out_ref[:, at : at + size] = dot(joined[...], buffer[:, at : at + size]).astype(BF16)


def expert_out(core, own, other, w_out):
    rows, half = own.shape
    hidden, width = w_out.shape
    edges = [width // 128 * i // 4 * 128 for i in range(5)]
    spans = [(at, to - at) for at, to in zip(edges, edges[1:])]
    return pl.pallas_call(
        functools.partial(expert_out_kernel, spans),
        in_specs=[SMEM, VMEM, VMEM, HBM],
        out_specs=VMEM,
        out_shape=shape(rows, width),
        scratch_shapes=[
            pltpu.VMEM((rows, hidden), BF16),
            pltpu.VMEM((hidden, width), BF16),
            pltpu.SemaphoreType.DMA((len(spans),)),
        ],
        compiler_params=params(16),
        cost_estimate=cost(5e9, 2 * width * hidden),
    )(core, own, other, in_hbm(w_out))


def join_halves(core_ref, own_ref, other_ref, joined):
    half = own_ref.shape[1]
    joined[:, pl.ds(aligned(core_ref[0], half), half)] = own_ref[...]
    joined[:, pl.ds(aligned(1 - core_ref[0], half), half)] = other_ref[...]


def grad_rows_kernel(steps, core_ref, own_ref, other_ref, w_ref, eo_ref, out_ref, joined, product):
    join_halves(core_ref, own_ref, other_ref, joined)
    rows = eo_ref.shape[0]
    width, _, hidden = w_ref.shape
    block = width // steps
    capacity = out_ref.shape[1] // 2
    chunks = rows // 128
    for i in range(steps):
        span = slice(i * block, (i + 1) * block)
        out = dot(w_ref[span].reshape(2 * block, hidden), joined[...], 1, 1)
        for j in range(2 * chunks):
            product[i % 2, j] = out[:, j * 128 : (j + 1) * 128]
        for j in range(chunks):
            gate = product[i % 2, j, pl.ds(0, block, stride=2), :]
            up = product[i % 2, chunks + j, pl.ds(1, block, stride=2), :]
            turned = (gate + up).T.astype(BF16).reshape(128 // capacity, capacity, block)
            kept = eo_ref[j * 128 : (j + 1) * 128, span].reshape(128 // capacity, capacity, block)
            both = jnp.concatenate([kept, turned], axis=1)
            out_ref[j * 128 // capacity : (j + 1) * 128 // capacity, :, span] = both


def grad_rows(core, own, other, w_in, out_rows, capacity):
    rows, width = out_rows.shape
    hidden = w_in.shape[2]
    steps = 7
    block = width // steps
    return pl.pallas_call(
        functools.partial(grad_rows_kernel, steps),
        in_specs=[SMEM, VMEM, VMEM, VMEM, VMEM],
        out_specs=VMEM,
        out_shape=shape(rows // capacity, 2 * capacity, width),
        scratch_shapes=[
            pltpu.VMEM((2 * rows, hidden), BF16),
            pltpu.VMEM((2, 2 * rows // 128, 2 * block, 128), F32),
        ],
        compiler_params=params(16),
        cost_estimate=cost(8 * rows * width * hidden, 4 * width * hidden),
    )(core, own, other, w_in, out_rows)


def write_blocks(buffer, sems, make, target):
    steps = buffer.shape[0]

    def copy(i):
        return pltpu.make_async_copy(buffer.at[i], target(i), sems.at[i])

    @pl.loop(0, steps)
    def _(i):
        buffer[i] = make(i)
        copy(i).start()

    @pl.loop(0, steps)
    def _(i):
        copy(i).wait()


def grad_in_kernel(core_ref, own_ref, other_ref, spread_ref, out_hbm, joined, buffer, sems):
    join_halves(core_ref, own_ref, other_ref, joined)
    block = buffer.shape[1]

    def make(i):
        part = spread_ref[:, pl.ds(aligned(i, 2 * block), 2 * block)]
        return dot(part, joined[...], 0, 0).astype(BF16).reshape(buffer.shape[1:])

    def target(i):
        return out_hbm.at[pl.ds(i * block, block)]

    write_blocks(buffer, sems, make, target)


def grad_in(core, own, other, spread):
    both, half = own.shape
    hidden = 2 * half
    width = spread.shape[1] // 2
    block = 128
    steps = width // block
    return pl.pallas_call(
        grad_in_kernel,
        in_specs=[SMEM, VMEM, VMEM, VMEM],
        out_specs=HBM,
        out_shape=shape(width, 2, hidden),
        scratch_shapes=[
            pltpu.VMEM((both, hidden), BF16),
            pltpu.VMEM((steps, block, 2, hidden), BF16),
            pltpu.SemaphoreType.DMA((steps,)),
        ],
        compiler_params=params(24),
        cost_estimate=cost(4 * both * width * hidden, 4 * width * hidden),
    )(core, own, other, spread)


def grad_out_kernel(core_ref, own_ref, other_ref, sc_ref, out_hbm, joined, buffer, sems):
    rows = own_ref.shape[0]
    join_halves(core_ref, own_ref, other_ref, joined)
    block, width = buffer.shape[1:]
    sc = sc_ref[...].reshape(rows, width)

    def make(i):
        return dot(joined[:, pl.ds(aligned(i, block), block)], sc, 0, 0).astype(BF16)

    def target(i):
        return out_hbm.at[pl.ds(aligned(i, block), block)]

    write_blocks(buffer, sems, make, target)


def grad_out(core, own, other, sc_in):
    rows, half = own.shape
    width = sc_in.shape[2]
    block = 256
    steps = 2 * half // block
    return pl.pallas_call(
        grad_out_kernel,
        in_specs=[SMEM, VMEM, VMEM, VMEM],
        out_specs=HBM,
        out_shape=shape(2 * half, width),
        scratch_shapes=[
            pltpu.VMEM((rows, 2 * half), BF16),
            pltpu.VMEM((steps, block, width), BF16),
            pltpu.SemaphoreType.DMA((steps,)),
        ],
        compiler_params=params(24),
        cost_estimate=cost(4 * rows * width * half, 4 * width * half),
    )(core, own, other, sc_in)


def to_tokens_kernel(experts, capacity, routes_ref, gate_ref, cot_ref, rows_hbm, out_ref, grad_ref, dprob_ref, rows, sems):
    width = rows_hbm.shape[2]
    parts = rows_hbm.shape[0] // experts

    def copy(r):
        span = pl.ds(r * experts, experts)
        return pltpu.make_async_copy(rows_hbm.at[span], rows.at[span], sems.at[r])

    for r in range(parts):
        copy(r).start()
    placed, prob = slot_tables(routes_ref, gate_ref, experts, capacity, 2)
    slot = lax.broadcasted_iota(jnp.int32, placed.shape, 0)
    first = slot % (2 * capacity) < capacity
    weight = jnp.where(placed & first, prob, 0.0).astype(BF16)
    place = jnp.where(placed & jnp.logical_not(first), 1.0, 0.0).astype(BF16)
    dots = jnp.zeros(placed.shape, F32)
    for r in range(parts):
        span = slice(r * width, (r + 1) * width)
        copy(r).wait()
        part = rows[r * experts : (r + 1) * experts].reshape(placed.shape[0], width)
        out_ref[:, span] = dot(weight, part, 0, 0).astype(BF16)
        grad_ref[:, span] = dot(place, part, 0, 0).astype(BF16)
        dots = dots + dot(part, cot_ref[:, span], 1, 1)
    dots = jnp.where(placed & first, dots, 0.0)
    expert = slot // (2 * capacity)
    for k in range(dprob_ref.shape[0]):
        term = jnp.where(routes_ref[k : k + 1, :] == expert, dots, 0.0)
        dprob_ref[k : k + 1, :] = jnp.sum(term, axis=0, keepdims=True)


def to_tokens(routes, gate_probs, cotangent, returned, experts, capacity):
    return pl.pallas_call(
        functools.partial(to_tokens_kernel, experts, capacity),
        in_specs=[VMEM, VMEM, VMEM, HBM],
        out_shape=(shape(*cotangent.shape), shape(*cotangent.shape), shape(*routes.shape, dtype=F32)),
        scratch_shapes=[
            pltpu.VMEM(returned.shape, BF16),
            pltpu.SemaphoreType.DMA((returned.shape[0] // experts,)),
        ],
        compiler_params=params(8),
        cost_estimate=cost(6 * returned.size * 8, 2 * returned.size),
    )(routes, gate_probs, cotangent, in_hbm(returned))


def on_device(tokens, routes, gate_probs, cotangent, w_gate_up, w_down):
    n_row = lax.axis_size("erow")
    experts = lax.axis_size("ecol")
    capacity = tokens.shape[0] // 2
    rows = n_row * experts * capacity
    core = (lax.axis_index("erow") % 2).astype(jnp.int32).reshape(1)
    routes, gate_probs = routes.T, gate_probs.T

    x_in = exchange(to_slots(routes, gate_probs, tokens, False, n_row, experts, capacity))
    sc_out = to_slots(routes, gate_probs, cotangent, True, n_row, experts, capacity)
    x_in, sc_out = lax.optimization_barrier((x_in, sc_out))
    sc_in = exchange(sc_out)
    w_in, w_out = w_gate_up[0], w_down[0]

    pre_send, pre_keep, spread = pre_halves(core, x_in, w_in, rows)
    pre_part, pre_others = sum_parts(pre_send, pre_keep)
    hid_send, hid_keep = down_t_halves(core, sc_in, w_out, rows)
    hid_part, hid_others = sum_parts(hid_send, hid_keep)

    pre_others, hid_part = lax.optimization_barrier((pre_others, hid_part))
    pre = total(pre_part, pre_others)
    gate, up = pre[:rows], pre[rows:]
    hidden_own, pre = lax.optimization_barrier(((gate * jax.nn.sigmoid(gate) * up).astype(BF16), pre))
    hidden_other = swap_cores(hidden_own)
    out_rows = expert_out(core, hidden_own, hidden_other, w_out)
    grad_down = grad_out(core, hidden_own, hidden_other, sc_in)[None]

    hid_others, out_rows = lax.optimization_barrier((hid_others, out_rows))
    grad_hidden = total(hid_part, hid_others)
    gate, up = pre[:rows], pre[rows:]
    s = jax.nn.sigmoid(gate)
    activated = gate * s
    grad_gate = grad_hidden * up * s * (1.0 + gate * (1.0 - s))
    grad_up = grad_hidden * activated
    grad_own = jnp.concatenate([grad_gate, grad_up], axis=0).astype(BF16)
    grad_other = swap_cores(grad_own)
    back = exchange(grad_rows(core, grad_own, grad_other, w_in, out_rows, capacity))
    grad_gate_up = grad_in(core, grad_own, grad_other, spread)[None]

    out, grad_tokens, grad_probs = to_tokens(routes, gate_probs, cotangent, back, experts, capacity)
    return (out, grad_tokens, grad_probs.T, grad_gate_up, grad_down)


def solution(mesh):
    flat = P(BOTH, None)
    return jax.shard_map(
        on_device,
        mesh=mesh,
        in_specs=(flat, flat, flat, flat, P("ecol", "erow", None, None), P("ecol", None, "erow")),
        out_specs=(flat, flat, flat, P("ecol", "erow", None, None), P("ecol", None, "erow")),
        check_vma=False,
    )
```

time: 216 us -> 104 us (0.48)
  matrix products: 52.1 us -> 0 us
  Pallas kernels: 0 us -> 42 us
  waiting for transfers between devices: 78.9 us -> 37.7 us
  local copies, waits for them, and re-layouts: 38.7 us -> 1.94 us
  between operations: 14.3 us -> 0.89 us
  starting transfers between devices: 25.6 us -> 18.7 us
  other arithmetic: 6.05 us -> 1.93 us
    dot_general x10 -> x0, matrix products: 52.1 us -> none  [the longest x1 15.3 us: on_device(): jnp.einsum('rd,dgf->rgf', x_rows, w_in, preferred_element_type=jnp.float32)]
    pallas_call x0 -> x9, Pallas kernels: none -> 42 us  [the longest x1 7.9 us: grad_in(): pl.pallas_call(grad_in_kernel, in_specs=[SMEM, VMEM, VMEM, VMEM], out_spe...]
    psum x1 -> x0, waiting for transfers between devices: 39.5 us -> none  [reduce_parts(): lax.psum(partial_term.astype(jnp.bfloat16), 'erow').astype(jnp.float32)]
    unnamed x18 -> x22, local copies, waits for them, and re-layouts: 27.5 us -> 1.94 us
    all_to_all x6 -> x3, waiting for transfers between devices: 39.4 us -> 27.4 us  [exchange(): return lax.all_to_all(rows, BOTH, split_axis=0, concat_axis=0, tiled=True)]
    all_to_all x6 -> x3, starting transfers between devices: 25.6 us -> 15.1 us  [exchange(): return lax.all_to_all(rows, BOTH, split_axis=0, concat_axis=0, tiled=True)]
    ppermute x0 -> x6, waiting for transfers between devices: none -> 10.3 us  [the longest x4 5.29 us: swap_cores(): return lax.ppermute(value, 'erow', [(i, i ^ 1) for i in range(n_row)])]
    reshape x9 -> x0, local copies, waits for them, and re-layouts: 6.98 us -> none  [the longest x2 3.16 us: send_rows(): x_in.reshape(-1, weight_slice)]
  transfers between devices with their start and end apart: 7 -> 9, of which waited for: 6 -> 9; matrix products, arithmetic and copies ran while one was open for 29% -> 0% of each run, Pallas kernels for 0% -> 30%
where the time goes in v2:
time: 104 us; the launch traced here: 103 us
  Pallas kernels  42 us (40%)
  waiting for transfers between devices  37.7 us (36%)
  starting transfers between devices  18.7 us (18%)
  local copies, waits for them, and re-layouts  1.94 us (2%)
  other arithmetic  1.93 us (2%)
    all_to_all x3, waiting for transfers between devices, exchange(): return lax.all_to_all(rows, BOTH, split_axis=0, concat_axis=0, tiled=True)  27.4 us
    all_to_all x3, starting transfers between devices, exchange(): return lax.all_to_all(rows, BOTH, split_axis=0, concat_axis=0, tiled=True)  15.1 us
    pallas_call x1, Pallas kernels, grad_in(): pl.pallas_call(grad_in_kernel, in_specs=[SMEM, VMEM, VMEM, VMEM], out_spe...  7.9 us
    pallas_call x1, Pallas kernels, pre_halves(): pl.pallas_call(pre_kernel, in_specs=[SMEM, VMEM, HBM], out_specs=[VMEM, V...  7 us
    pallas_call x1, Pallas kernels, grad_rows(): pl.pallas_call(functools.partial(grad_rows_kernel, steps), in_specs=[SMEM...  6.3 us
    ppermute x4, waiting for transfers between devices, swap_cores(): return lax.ppermute(value, 'erow', [(i, i ^ 1) for i in range(n_row)])  5.29 us
    ppermute x2, waiting for transfers between devices, sum_parts(): others.append(lax.ppermute(chip_sum, 'erow', perm))  5.01 us
    pallas_call x1, Pallas kernels, down_t_halves(): pl.pallas_call(down_t_kernel, in_specs=[SMEM, VMEM, HBM], out_specs=[VMEM...  4.84 us
  transfers between devices with their start and end apart: 9, of which 9 were waited for; matrix products, arithmetic and copies ran while one was open for 0% of the time, Pallas kernels for 30%

profile of v2, /device:TPU:0, one launch (start us, length us, event | category | flops | bytes accessed | tf_op | source)
XLA Modules:
  0.0 103.1 jit_solution(11322831613442217857)
XLA Ops:
  0.6 2.0 %shard_map.101 = bf16[32,4,1792]{2,1,0:T(4,128)(2,1)} custom-call(s32[4,8]{1,0:T(4,128)} %bitcast.12, bf16[4,8]{1,0:T(4,128)(2,1)} %bitcast.15, bf16[8,7168]{1,0:T(8,128)(2,1)} %rows_hbm.2), custom_call_target="tpu_custom_call" | custom-call | flops 3670016 | bytes 114688 | tf_op jit(solution)/shard_map/pallas_call | solution.py:83
  2.6 7.3 %all-to-all-start = ((bf16[32,4,1792]{2,1,0:T(4,128)(2,1)}), bf16[32,4,1792]{2,1,0:T(4,128)(2,1)S(1)}, u32[]{:S(2)}, u32[]{:S(2)}) async-start(bf16[32,4,1792]{2,1,0:T(4,128)(2,1)} %shard_map.101), calls=%async_computation | async-start | bytes 917504 | tf_op jit(solution)/shard_map/all_to_all | solution.py:99
  9.9 2.0 %shard_map.102 = bf16[32,4,1792]{2,1,0:T(4,128)(2,1)} custom-call(s32[4,8]{1,0:T(4,128)} %bitcast.13, bf16[4,8]{1,0:T(4,128)(2,1)} %bitcast.16, bf16[8,7168]{1,0:T(8,128)(2,1)} %cot_ref.1), custom_call_target="tpu_custom_call" | custom-call | flops 3670016 | bytes 114688 | tf_op jit(solution)/shard_map/pallas_call | solution.py:83
  11.9 13.0 %all-to-all-done.x_ref = bf16[32,4,1792]{2,1,0:T(4,128)(2,1)S(1)} async-done(((bf16[32,4,1792]{2,1,0:T(4,128)(2,1)}), bf16[32,4,1792]{2,1,0:T(4,128)(2,1)S(1)}, u32[]{:S(2)}, u32[]{:S(2)}) %all-to-all-start) | async-done | bytes 458784 | tf_op jit(solution)/shard_map/all_to_all | solution.py:99
  24.9 2.6 %all-to-all-start.1 = ((bf16[32,4,1792]{2,1,0:T(4,128)(2,1)}), bf16[32,4,1792]{2,1,0:T(4,128)(2,1)S(1)}, u32[]{:S(2)}, u32[]{:S(2)}) async-start(bf16[32,4,1792]{2,1,0:T(4,128)(2,1)} %shard_map.102), calls=%async_computation.1 | async-start | bytes 917504 | tf_op jit(solution)/shard_map/all_to_all | solution.py:99
  27.5 7.0 %shard_map.103 = (bf16[256,1024]{1,0:T(8,128)(2,1)S(1)}, f32[256,1024]{1,0:T(8,128)S(1)}, bf16[256,3584]{1,0:T(8,128)(2,1)S(1)}) custom-call(s32[1]{0:T(128)} %bitcast.2.core_ref, bf16[32,4,1792]{2,1,0:T(4,128)(2,1)S(1)} %all-to-all-done.x_ref, bf16[1792,2,2048]{2,1,0:T(2,128)(2,1)} %bitcast.8), custom_call_target="tpu_custom_call" | custom-call | flops 10000000000 | bytes 14680064 | tf_op jit(solution)/shard_map/pallas_call | solution.py:147
  34.5 0.2 collective-permute-start
  34.7 1.8 %collective-permute-done = bf16[256,1024]{1,0:T(8,128)(2,1)S(1)} collective-permute-done((bf16[256,1024]{1,0:T(8,128)(2,1)S(1)}, bf16[256,1024]{1,0:T(8,128)(2,1)S(1)}, u32[]{:S(2)}, u32[]{:S(2)}) %collective-permute-start) | collective-permute-done | bytes 524320 | tf_op jit(solution)/shard_map/ppermute | solution.py:203
  36.5 0.2 add_convert_fusion
  36.6 1.7 %collective-permute-start.1 = (bf16[256,1024]{1,0:T(8,128)(2,1)S(1)}, bf16[256,1024]{1,0:T(8,128)(2,1)}, u32[]{:S(2)}, u32[]{:S(2)}) collective-permute-start(bf16[256,1024]{1,0:T(8,128)(2,1)S(1)} %add_convert_fusion), channel_id=1, source_target_pairs={{0,16},{8,24},{16,0},{24,8},{1,17},{9,25},{17,1},{25,9},{2,18},{10... | collective-permute-start | bytes 1572872 | tf_op jit(solution)/shard_map/ppermute | solution.py:213
  38.3 4.1 %all-to-all-done.1.sc_ref = bf16[32,4,1792]{2,1,0:T(4,128)(2,1)S(1)} async-done(((bf16[32,4,1792]{2,1,0:T(4,128)(2,1)}), bf16[32,4,1792]{2,1,0:T(4,128)(2,1)S(1)}, u32[]{:S(2)}, u32[]{:S(2)}) %all-to-all-start.1) | async-done | bytes 458784 | tf_op jit(solution)/shard_map/all_to_all | solution.py:99
  42.4 4.8 %shard_map.104 = (bf16[128,1024]{1,0:T(8,128)(2,1)S(1)}, f32[128,1024]{1,0:T(8,128)S(1)}) custom-call(s32[1]{0:T(128)} %bitcast.2.core_ref, bf16[32,4,1792]{2,1,0:T(4,128)(2,1)S(1)} %all-to-all-done.1.sc_ref, bf16[2048,1792]{1,0:T(8,128)(2,1)} %bitcast.19), custom_call_target="tpu_custom_call" | custom-call | flops 939524096 | bytes 7340032 | tf_op jit(solution)/shard_map/pallas_call | solution.py:187
  47.3 0.1 collective-permute-start.2
  47.4 1.5 %collective-permute-done.2 = bf16[128,1024]{1,0:T(8,128)(2,1)S(1)} collective-permute-done((bf16[128,1024]{1,0:T(8,128)(2,1)S(1)}, bf16[128,1024]{1,0:T(8,128)(2,1)S(1)}, u32[]{:S(2)}, u32[]{:S(2)}) %collective-permute-start.2) | collective-permute-done | bytes 262176 | tf_op jit(solution)/shard_map/ppermute | solution.py:203
  49.0 2.5 %collective-permute-done.1 = bf16[256,1024]{1,0:T(8,128)(2,1)} collective-permute-done((bf16[256,1024]{1,0:T(8,128)(2,1)S(1)}, bf16[256,1024]{1,0:T(8,128)(2,1)}, u32[]{:S(2)}, u32[]{:S(2)}) %collective-permute-start.1) | collective-permute-done | bytes 524320 | tf_op jit(solution)/shard_map/ppermute | solution.py:213
  51.5 1.2 %convert_add_fusion = f32[256,1024]{1,0:T(8,128)S(1)} fusion(bf16[256,1024]{1,0:T(8,128)(2,1)} %collective-permute-done.1, bf16[256,1024]{1,0:T(8,128)(2,1)S(1)} %add_convert_fusion), kind=kLoop, calls=%fused_computation | loop fusion | flops 786432 | bytes 2097152 | tf_op jit(solution)/shard_map/add | solution.py:220
  52.7 0.2 fusion.own_ref
  52.9 0.1 collective-permute-start.4
  53.0 1.5 %collective-permute-start.3 = (bf16[128,1024]{1,0:T(8,128)(2,1)S(1)}, bf16[128,1024]{1,0:T(8,128)(2,1)S(1)}, u32[]{:S(2)}, u32[]{:S(2)}) collective-permute-start(bf16[128,1024]{1,0:T(8,128)(2,1)S(1)} %add_convert_fusion.1), channel_id=1, source_target_pairs={{0,16},{8,24},{16,0},{24,8},{1,17},{9,25},{17,1},{25,9},{2,18},{10... | collective-permute-start | bytes 786440 | tf_op jit(solution)/shard_map/ppermute | solution.py:213
  54.5 4.7 %shard_map.105.eo_ref = bf16[128,1792]{1,0:T(8,128)(2,1)S(1)} custom-call(s32[1]{0:T(128)} %bitcast.2.core_ref, bf16[128,1024]{1,0:T(8,128)(2,1)S(1)} %fusion.own_ref, bf16[128,1024]{1,0:T(8,128)(2,1)S(1)} %collective-permute-done.4.other_ref, bf16[2048,1792]{1,0:T(8,128)(2,1)} %bitcast.20), custom_call_target="tpu_custom_call" | custom-call | flops 5000000000 | bytes 7340032 | tf_op jit(solution)/shard_map/pallas_call | solution.py:241
  59.3 2.5 %collective-permute-done.3 = bf16[128,1024]{1,0:T(8,128)(2,1)S(1)} collective-permute-done((bf16[128,1024]{1,0:T(8,128)(2,1)S(1)}, bf16[128,1024]{1,0:T(8,128)(2,1)S(1)}, u32[]{:S(2)}, u32[]{:S(2)}) %collective-permute-start.3) | collective-permute-done | bytes 262176 | tf_op jit(solution)/shard_map/ppermute | solution.py:213
  61.7 0.3 multiply_convert_fusion.1
  62.1 0.1 collective-permute-start.5
  62.2 1.9 %collective-permute-done.5.other_ref = bf16[256,1024]{1,0:T(8,128)(2,1)S(1)} collective-permute-done((bf16[256,1024]{1,0:T(8,128)(2,1)S(1)}, bf16[256,1024]{1,0:T(8,128)(2,1)S(1)}, u32[]{:S(2)}, u32[]{:S(2)}) %collective-permute-start.5) | collective-permute-done | bytes 524320 | tf_op jit(solution)/shard_map/ppermute | solution.py:203
  64.1 6.3 %shard_map.106 = bf16[32,8,1792]{2,1,0:T(8,128)(2,1)} custom-call(s32[1]{0:T(128)} %bitcast.2.core_ref, bf16[256,1024]{1,0:T(8,128)(2,1)S(1)} %pad_maximum_fusion.own_ref, bf16[256,1024]{1,0:T(8,128)(2,1)S(1)} %collective-permute-done.5.other_ref, bf16[1792,2,2048]{2,1,0:T(2,128)(2,1)S(1)} %bitcast.11, bf16[128,1792]{1,0:T(8,128)(2,1)S(1)} %shard_map.105.eo_ref), custom_call_target="tpu_custom_call" | custom-call | flops 3758096384 | bytes 14680064 | tf_op jit(solution)/shard_map/pallas_call | solution.py:288
  70.4 5.2 %all-to-all-start.2 = ((bf16[32,8,1792]{2,1,0:T(8,128)(2,1)}), bf16[32,8,1792]{2,1,0:T(8,128)(2,1)}, u32[]{:S(2)}, u32[]{:S(2)}) async-start(bf16[32,8,1792]{2,1,0:T(8,128)(2,1)} %shard_map.106), calls=%async_computation.2 | async-start | bytes 1835008 | tf_op jit(solution)/shard_map/all_to_all | solution.py:99
  75.6 0.9 copy-done.1
  76.6 0.9 copy-done.4
  77.5 4.6 %shard_map.109 = bf16[2048,1792]{1,0:T(8,128)(2,1)} custom-call(s32[1]{0:T(128)} %bitcast.2.core_ref, bf16[128,1024]{1,0:T(8,128)(2,1)S(1)} %copy-done.1, bf16[128,1024]{1,0:T(8,128)(2,1)S(1)} %copy-done.4, bf16[32,4,1792]{2,1,0:T(4,128)(2,1)S(1)} %all-to-all-done.1.sc_ref), custom_call_target="tpu_custom_call" | custom-call | flops 939524096 | bytes 7340032 | tf_op jit(solution)/shard_map/pallas_call | solution.py:373
  82.2 7.9 %shard_map.108 = bf16[1792,2,2048]{2,1,0:T(2,128)(2,1)} custom-call(s32[1]{0:T(128)} %bitcast.2.core_ref, bf16[256,1024]{1,0:T(8,128)(2,1)S(1)} %pad_maximum_fusion.own_ref, bf16[256,1024]{1,0:T(8,128)(2,1)S(1)} %collective-permute-done.5.other_ref, bf16[256,3584]{1,0:T(8,128)(2,1)S(1)} %get-tuple-element.36.spread_ref), custom_call_target="tpu_custom_call" | custom-call | flops 3758096384 | bytes 14680064 | tf_op jit(solution)/shard_map/pallas_call | solution.py:338
  90.1 10.3 %all-to-all-done.2.rows_hbm = bf16[32,8,1792]{2,1,0:T(8,128)(2,1)} async-done(((bf16[32,8,1792]{2,1,0:T(8,128)(2,1)}), bf16[32,8,1792]{2,1,0:T(8,128)(2,1)}, u32[]{:S(2)}, u32[]{:S(2)}) %all-to-all-start.2) | async-done | bytes 917536 | tf_op jit(solution)/shard_map/all_to_all | solution.py:99
  100.4 2.6 %shard_map.107 = (bf16[8,7168]{1,0:T(8,128)(2,1)}, bf16[8,7168]{1,0:T(8,128)(2,1)}, f32[4,8]{1,0:T(4,128)}) custom-call(s32[4,8]{1,0:T(4,128)S(1)} %bitcast.14, bf16[4,8]{1,0:T(4,128)(2,1)S(1)} %bitcast.17, bf16[8,7168]{1,0:T(8,128)(2,1)S(1)} %copy-done.2, bf16[32,8,1792]{2,1,0:T(8,128)(2,1)} %all-to-all-done.2.rows_hbm), custom_call_target="tpu_custom_call" | custom-call | flops 22020096 | bytes 917504 | tf_op jit(solution)/shard_map/pallas_call | solution.py:419
  (24 shorter events, 0.2 us)
Async XLA Ops:
  2.6 22.3 %all-to-all-start = ((bf16[32,4,1792]{2,1,0:T(4,128)(2,1)}), bf16[32,4,1792]{2,1,0:T(4,128)(2,1)S(1)}, u32[]{:S(2)}, u32[]{:S(2)}) async-start(bf16[32,4,1792]{2,1,0:T(4,128)(2,1)} %shard_map.101), calls=%async_computation | async-start | bytes 917504 | tf_op jit(solution)/shard_map/all_to_all | solution.py:99
  24.9 17.6 %all-to-all-start.1 = ((bf16[32,4,1792]{2,1,0:T(4,128)(2,1)}), bf16[32,4,1792]{2,1,0:T(4,128)(2,1)S(1)}, u32[]{:S(2)}, u32[]{:S(2)}) async-start(bf16[32,4,1792]{2,1,0:T(4,128)(2,1)} %shard_map.102), calls=%async_computation.1 | async-start | bytes 917504 | tf_op jit(solution)/shard_map/all_to_all | solution.py:99
  34.5 2.0 %collective-permute-start = (bf16[256,1024]{1,0:T(8,128)(2,1)S(1)}, bf16[256,1024]{1,0:T(8,128)(2,1)S(1)}, u32[]{:S(2)}, u32[]{:S(2)}) collective-permute-start(bf16[256,1024]{1,0:T(8,128)(2,1)S(1)} %get-tuple-element.23), channel_id=1, source_target_pairs={{0,8},{8,0},{16,24},{24,16},{1,9},{9,1},{17,25},{25,17},{2,10},{10... | collective-permute-start | bytes 1572872 | tf_op jit(solution)/shard_map/ppermute | solution.py:203
  36.6 14.9 %collective-permute-start.1 = (bf16[256,1024]{1,0:T(8,128)(2,1)S(1)}, bf16[256,1024]{1,0:T(8,128)(2,1)}, u32[]{:S(2)}, u32[]{:S(2)}) collective-permute-start(bf16[256,1024]{1,0:T(8,128)(2,1)S(1)} %add_convert_fusion), channel_id=1, source_target_pairs={{0,16},{8,24},{16,0},{24,8},{1,17},{9,25},{17,1},{25,9},{2,18},{10... | collective-permute-start | bytes 1572872 | tf_op jit(solution)/shard_map/ppermute | solution.py:213
  42.4 21.6 %slice-start = ((s8[14680064]{0:T(1024)(128)(4,1)}), s8[4194304]{0:T(1024)(128)(4,1)S(1)}, s32[]{:S(2)}) async-start(s8[14680064]{0:T(1024)(128)(4,1)} %bitcast.9), calls=%async_computation.3 | async-start | bytes 8388608
  47.3 1.6 %collective-permute-start.2 = (bf16[128,1024]{1,0:T(8,128)(2,1)S(1)}, bf16[128,1024]{1,0:T(8,128)(2,1)S(1)}, u32[]{:S(2)}, u32[]{:S(2)}) collective-permute-start(bf16[128,1024]{1,0:T(8,128)(2,1)S(1)} %get-tuple-element.26), channel_id=1, source_target_pairs={{0,8},{8,0},{16,24},{24,16},{1,9},{9,1},{17,25},{25,17},{2,10},{10... | collective-permute-start | bytes 786440 | tf_op jit(solution)/shard_map/ppermute | solution.py:203
  48.9 15.2 %slice-start.1 = ((s8[14680064]{0:T(1024)(128)(4,1)}), s8[4194304]{0:T(1024)(128)(4,1)S(1)}, s32[]{:S(2)}) async-start(s8[14680064]{0:T(1024)(128)(4,1)} %bitcast.9), calls=%async_computation.4 | async-start | bytes 8388608
  52.9 6.4 %copy-start = (bf16[128,1024]{1,0:T(8,128)(2,1)}, bf16[128,1024]{1,0:T(8,128)(2,1)S(1)}, u32[]{:S(2)}) copy-start(bf16[128,1024]{1,0:T(8,128)(2,1)S(1)} %fusion.own_ref) | copy-start | bytes 786436
  52.9 11.2 %slice-start.2 = ((s8[14680064]{0:T(1024)(128)(4,1)}), s8[4194304]{0:T(1024)(128)(4,1)S(1)}, s32[]{:S(2)}) async-start(s8[14680064]{0:T(1024)(128)(4,1)} %bitcast.9), calls=%async_computation.5 | async-start | bytes 8388608
  52.9 11.2 %slice-start.3 = ((s8[14680064]{0:T(1024)(128)(4,1)}), s8[2097152]{0:T(1024)(128)(4,1)S(1)}, s32[]{:S(2)}) async-start(s8[14680064]{0:T(1024)(128)(4,1)} %bitcast.9), calls=%async_computation.6 | async-start | bytes 4194304
  52.9 1.6 %collective-permute-start.4 = (bf16[128,1024]{1,0:T(8,128)(2,1)S(1)}, bf16[128,1024]{1,0:T(8,128)(2,1)S(1)}, u32[]{:S(2)}, u32[]{:S(2)}) collective-permute-start(bf16[128,1024]{1,0:T(8,128)(2,1)S(1)} %fusion.own_ref), channel_id=1, source_target_pairs={{0,8},{8,0},{16,24},{24,16},{1,9},{9,1},{17,25},{25,17},{2,10},{10... | collective-permute-start | bytes 786440 | tf_op jit(solution)/shard_map/ppermute | solution.py:203
  53.0 8.7 %collective-permute-start.3 = (bf16[128,1024]{1,0:T(8,128)(2,1)S(1)}, bf16[128,1024]{1,0:T(8,128)(2,1)S(1)}, u32[]{:S(2)}, u32[]{:S(2)}) collective-permute-start(bf16[128,1024]{1,0:T(8,128)(2,1)S(1)} %add_convert_fusion.1), channel_id=1, source_target_pairs={{0,16},{8,24},{16,0},{24,8},{1,17},{9,25},{17,1},{25,9},{2,18},{10... | collective-permute-start | bytes 786440 | tf_op jit(solution)/shard_map/ppermute | solution.py:213
  54.5 4.7 %copy-start.3 = (bf16[128,1024]{1,0:T(8,128)(2,1)}, bf16[128,1024]{1,0:T(8,128)(2,1)S(1)}, u32[]{:S(2)}) copy-start(bf16[128,1024]{1,0:T(8,128)(2,1)S(1)} %collective-permute-done.4.other_ref) | copy-start | bytes 786436
  62.1 2.0 %collective-permute-start.5 = (bf16[256,1024]{1,0:T(8,128)(2,1)S(1)}, bf16[256,1024]{1,0:T(8,128)(2,1)S(1)}, u32[]{:S(2)}, u32[]{:S(2)}) collective-permute-start(bf16[256,1024]{1,0:T(8,128)(2,1)S(1)} %pad_maximum_fusion.own_ref), channel_id=1, source_target_pairs={{0,8},{8,0},{16,24},{24,16},{1,9},{9,1},{17,25},{25,17},{2,10},{10... | collective-permute-start | bytes 1572872 | tf_op jit(solution)/shard_map/ppermute | solution.py:203
  70.4 30.0 %all-to-all-start.2 = ((bf16[32,8,1792]{2,1,0:T(8,128)(2,1)}), bf16[32,8,1792]{2,1,0:T(8,128)(2,1)}, u32[]{:S(2)}, u32[]{:S(2)}) async-start(bf16[32,8,1792]{2,1,0:T(8,128)(2,1)} %shard_map.106), calls=%async_computation.2 | async-start | bytes 1835008 | tf_op jit(solution)/shard_map/all_to_all | solution.py:99
  75.6 1.0 copy-start.1
  76.6 0.9 copy-start.4
  82.2 18.3 %copy-start.2 = (bf16[8,7168]{1,0:T(8,128)(2,1)S(1)}, bf16[8,7168]{1,0:T(8,128)(2,1)}, u32[]{:S(2)}) copy-start(bf16[8,7168]{1,0:T(8,128)(2,1)} %cot_ref.1) | copy-start | bytes 344068
  82.2 18.2 %copy-start.5 = (s32[8,4]{0,1:T(4,128)S(1)}, s32[8,4]{0,1:T(4,128)}, u32[]{:S(2)}) copy-start(s32[8,4]{0,1:T(4,128)} %param.7) | copy-start | bytes 388
  82.2 18.2 %copy-start.6 = (bf16[8,4]{0,1:T(4,128)(2,1)S(1)}, bf16[8,4]{0,1:T(4,128)(2,1)}, u32[]{:S(2)}) copy-start(bf16[8,4]{0,1:T(4,128)(2,1)} %param.8) | copy-start | bytes 196

commit v3 on v2

--- a/solution.py
+++ b/solution.py
@@ -219,6 +219,25 @@
     for other in others:
         out = out + other.astype(F32)
     return out
+
+
+def hidden_kernel(*refs):
+    rows = refs[-1].shape[0]
+    pre = refs[0][...].astype(F32)
+    for ref in refs[1:-1]:
+        pre = pre + ref[...].astype(F32)
+    gate, up = pre[:rows], pre[rows:]
+    refs[-1][...] = (gate * jax.nn.sigmoid(gate) * up).astype(BF16)
+
+
+def hidden_half(part, others):
+    both, half = part.shape
+    return pl.pallas_call(
+        hidden_kernel,
+        out_shape=shape(both // 2, half),
+        compiler_params=params(6),
+        cost_estimate=cost(6 * part.size, 4 * part.size),
+    )(part, *others)
 
 
 def expert_out_kernel(spans, core_ref, own_ref, other_ref, w_hbm, out_ref, joined, buffer, sems):
@@ -449,15 +468,14 @@
     hid_part, hid_others = sum_parts(hid_send, hid_keep)
 
     pre_others, hid_part = lax.optimization_barrier((pre_others, hid_part))
-    pre = total(pre_part, pre_others)
-    gate, up = pre[:rows], pre[rows:]
-    hidden_own, pre = lax.optimization_barrier(((gate * jax.nn.sigmoid(gate) * up).astype(BF16), pre))
+    hidden_own = hidden_half(pre_part, pre_others)
     hidden_other = swap_cores(hidden_own)
     out_rows = expert_out(core, hidden_own, hidden_other, w_out)
     grad_down = grad_out(core, hidden_own, hidden_other, sc_in)[None]
 
     hid_others, out_rows = lax.optimization_barrier((hid_others, out_rows))
     grad_hidden = total(hid_part, hid_others)
+    pre = total(pre_part, pre_others)
     gate, up = pre[:rows], pre[rows:]
     s = jax.nn.sigmoid(gate)
     activated = gate * s

time: 104 us -> 101 us (0.971)
  waiting for transfers between devices: 37.7 us -> 35.7 us
  other arithmetic: 1.93 us -> 0.73 us
    ppermute x2, waiting for transfers between devices: 5.01 us -> 1.84 us  [sum_parts(): others.append(lax.ppermute(chip_sum, 'erow', perm))]
    ppermute x4, waiting for transfers between devices: 5.29 us -> 6.5 us  [swap_cores(): return lax.ppermute(value, 'erow', [(i, i ^ 1) for i in range(n_row)])]
    add x1, other arithmetic: 1.21 us -> 0.17 us  [total(): out = out + other.astype(F32)]
  transfers between devices with their start and end apart: 9 -> 9, of which waited for: 9 -> 8; matrix products, arithmetic and copies ran while one was open for 0% -> 0% of each run, Pallas kernels for 30% -> 31%
where the time goes in v3:
time: 101 us; the launch traced here: 100 us
  Pallas kernels  42.3 us (42%)
  waiting for transfers between devices  35.7 us (35%)
  starting transfers between devices  18.7 us (19%)
  local copies, waits for them, and re-layouts  1.94 us (2%)
    all_to_all x3, waiting for transfers between devices, exchange(): return lax.all_to_all(rows, BOTH, split_axis=0, concat_axis=0, tiled=True)  27.4 us
    all_to_all x3, starting transfers between devices, exchange(): return lax.all_to_all(rows, BOTH, split_axis=0, concat_axis=0, tiled=True)  15.9 us
    pallas_call x1, Pallas kernels, grad_in(): pl.pallas_call(grad_in_kernel, in_specs=[SMEM, VMEM, VMEM, VMEM], out_spe...  7.9 us
    pallas_call x1, Pallas kernels, pre_halves(): pl.pallas_call(pre_kernel, in_specs=[SMEM, VMEM, HBM], out_specs=[VMEM, V...  7 us
    ppermute x4, waiting for transfers between devices, swap_cores(): return lax.ppermute(value, 'erow', [(i, i ^ 1) for i in range(n_row)])  6.5 us
    pallas_call x1, Pallas kernels, grad_rows(): pl.pallas_call(functools.partial(grad_rows_kernel, steps), in_specs=[SMEM...  6.3 us
    pallas_call x1, Pallas kernels, expert_out(): pl.pallas_call(functools.partial(expert_out_kernel, spans), in_specs=[SME...  4.9 us
    pallas_call x1, Pallas kernels, down_t_halves(): pl.pallas_call(down_t_kernel, in_specs=[SMEM, VMEM, HBM], out_specs=[VMEM...  4.84 us
  transfers between devices with their start and end apart: 9, of which 8 were waited for; matrix products, arithmetic and copies ran while one was open for 0% of the time, Pallas kernels for 31%

profile of v3, /device:TPU:0, one launch (start us, length us, event | category | flops | bytes accessed | tf_op | source)
XLA Modules:
  0.0 100.3 jit_solution(11093956814304898145)
XLA Ops:
  0.6 2.0 %shard_map.101 = bf16[32,4,1792]{2,1,0:T(4,128)(2,1)} custom-call(s32[4,8]{1,0:T(4,128)} %bitcast.12, bf16[4,8]{1,0:T(4,128)(2,1)} %bitcast.15, bf16[8,7168]{1,0:T(8,128)(2,1)} %rows_hbm.2), custom_call_target="tpu_custom_call" | custom-call | flops 3670016 | bytes 114688 | tf_op jit(solution)/shard_map/pallas_call | solution.py:83
  2.6 7.3 %all-to-all-start = ((bf16[32,4,1792]{2,1,0:T(4,128)(2,1)}), bf16[32,4,1792]{2,1,0:T(4,128)(2,1)S(1)}, u32[]{:S(2)}, u32[]{:S(2)}) async-start(bf16[32,4,1792]{2,1,0:T(4,128)(2,1)} %shard_map.101), calls=%async_computation | async-start | bytes 917504 | tf_op jit(solution)/shard_map/all_to_all | solution.py:99
  9.9 2.0 %shard_map.102 = bf16[32,4,1792]{2,1,0:T(4,128)(2,1)} custom-call(s32[4,8]{1,0:T(4,128)} %bitcast.13, bf16[4,8]{1,0:T(4,128)(2,1)} %bitcast.16, bf16[8,7168]{1,0:T(8,128)(2,1)} %cot_ref.1), custom_call_target="tpu_custom_call" | custom-call | flops 3670016 | bytes 114688 | tf_op jit(solution)/shard_map/pallas_call | solution.py:83
  11.9 13.0 %all-to-all-done.x_ref = bf16[32,4,1792]{2,1,0:T(4,128)(2,1)S(1)} async-done(((bf16[32,4,1792]{2,1,0:T(4,128)(2,1)}), bf16[32,4,1792]{2,1,0:T(4,128)(2,1)S(1)}, u32[]{:S(2)}, u32[]{:S(2)}) %all-to-all-start) | async-done | bytes 458784 | tf_op jit(solution)/shard_map/all_to_all | solution.py:99
  24.9 2.6 %all-to-all-start.1 = ((bf16[32,4,1792]{2,1,0:T(4,128)(2,1)}), bf16[32,4,1792]{2,1,0:T(4,128)(2,1)S(1)}, u32[]{:S(2)}, u32[]{:S(2)}) async-start(bf16[32,4,1792]{2,1,0:T(4,128)(2,1)} %shard_map.102), calls=%async_computation.1 | async-start | bytes 917504 | tf_op jit(solution)/shard_map/all_to_all | solution.py:99
  27.5 7.0 %shard_map.103 = (bf16[256,1024]{1,0:T(8,128)(2,1)S(1)}, f32[256,1024]{1,0:T(8,128)S(1)}, bf16[256,3584]{1,0:T(8,128)(2,1)S(1)}) custom-call(s32[1]{0:T(128)} %bitcast.2.core_ref, bf16[32,4,1792]{2,1,0:T(4,128)(2,1)S(1)} %all-to-all-done.x_ref, bf16[1792,2,2048]{2,1,0:T(2,128)(2,1)} %bitcast.8), custom_call_target="tpu_custom_call" | custom-call | flops 10000000000 | bytes 14680064 | tf_op jit(solution)/shard_map/pallas_call | solution.py:147
  34.5 0.2 collective-permute-start
  34.7 1.8 %collective-permute-done = bf16[256,1024]{1,0:T(8,128)(2,1)S(1)} collective-permute-done((bf16[256,1024]{1,0:T(8,128)(2,1)S(1)}, bf16[256,1024]{1,0:T(8,128)(2,1)S(1)}, u32[]{:S(2)}, u32[]{:S(2)}) %collective-permute-start) | collective-permute-done | bytes 524320 | tf_op jit(solution)/shard_map/ppermute | solution.py:203
  36.5 0.2 add_convert_fusion.refs_0_
  36.6 1.7 %collective-permute-start.1 = (bf16[256,1024]{1,0:T(8,128)(2,1)S(1)}, bf16[256,1024]{1,0:T(8,128)(2,1)S(1)}, u32[]{:S(2)}, u32[]{:S(2)}) collective-permute-start(bf16[256,1024]{1,0:T(8,128)(2,1)S(1)} %add_convert_fusion.refs_0_), channel_id=1, source_target_pairs={{0,16},{8,24},{16,0},{24,8},{1,17},{9,25},{17,1},{25,9},{2,18},{10... | collective-permute-start | bytes 1572872 | tf_op jit(solution)/shard_map/ppermute | solution.py:213
  38.3 4.1 %all-to-all-done.1.sc_ref = bf16[32,4,1792]{2,1,0:T(4,128)(2,1)S(1)} async-done(((bf16[32,4,1792]{2,1,0:T(4,128)(2,1)}), bf16[32,4,1792]{2,1,0:T(4,128)(2,1)S(1)}, u32[]{:S(2)}, u32[]{:S(2)}) %all-to-all-start.1) | async-done | bytes 458784 | tf_op jit(solution)/shard_map/all_to_all | solution.py:99
  42.4 4.8 %shard_map.104 = (bf16[128,1024]{1,0:T(8,128)(2,1)S(1)}, f32[128,1024]{1,0:T(8,128)S(1)}) custom-call(s32[1]{0:T(128)} %bitcast.2.core_ref, bf16[32,4,1792]{2,1,0:T(4,128)(2,1)S(1)} %all-to-all-done.1.sc_ref, bf16[2048,1792]{1,0:T(8,128)(2,1)} %bitcast.19), custom_call_target="tpu_custom_call" | custom-call | flops 939524096 | bytes 7340032 | tf_op jit(solution)/shard_map/pallas_call | solution.py:187
  47.3 0.1 collective-permute-start.2
  47.4 1.5 %collective-permute-done.2 = bf16[128,1024]{1,0:T(8,128)(2,1)S(1)} collective-permute-done((bf16[128,1024]{1,0:T(8,128)(2,1)S(1)}, bf16[128,1024]{1,0:T(8,128)(2,1)S(1)}, u32[]{:S(2)}, u32[]{:S(2)}) %collective-permute-start.2) | collective-permute-done | bytes 262176 | tf_op jit(solution)/shard_map/ppermute | solution.py:203
  48.9 0.6 collective-permute-start.3
  49.6 1.8 %collective-permute-done.1.refs_1_ = bf16[256,1024]{1,0:T(8,128)(2,1)S(1)} collective-permute-done((bf16[256,1024]{1,0:T(8,128)(2,1)S(1)}, bf16[256,1024]{1,0:T(8,128)(2,1)S(1)}, u32[]{:S(2)}, u32[]{:S(2)}) %collective-permute-start.1) | collective-permute-done | bytes 524320 | tf_op jit(solution)/shard_map/ppermute | solution.py:213
  51.4 0.2 shard_map.105.own_ref
  51.6 0.1 collective-permute-start.4
  51.7 0.2 convert_add_fusion
  51.9 1.3 %collective-permute-done.4.other_ref = bf16[128,1024]{1,0:T(8,128)(2,1)S(1)} collective-permute-done((bf16[128,1024]{1,0:T(8,128)(2,1)S(1)}, bf16[128,1024]{1,0:T(8,128)(2,1)S(1)}, u32[]{:S(2)}, u32[]{:S(2)}) %collective-permute-start.4) | collective-permute-done | bytes 262176 | tf_op jit(solution)/shard_map/ppermute | solution.py:203
  53.2 4.9 %shard_map.106.eo_ref = bf16[128,1792]{1,0:T(8,128)(2,1)S(1)} custom-call(s32[1]{0:T(128)} %bitcast.2.core_ref, bf16[128,1024]{1,0:T(8,128)(2,1)S(1)} %shard_map.105.own_ref, bf16[128,1024]{1,0:T(8,128)(2,1)S(1)} %collective-permute-done.4.other_ref, bf16[2048,1792]{1,0:T(8,128)(2,1)} %bitcast.20), custom_call_target="tpu_custom_call" | custom-call | flops 5000000000 | bytes 7340032 | tf_op jit(solution)/shard_map/pallas_call | solution.py:260
  58.1 0.3 fusion.2
  58.5 0.1 collective-permute-start.5
  58.6 1.9 %collective-permute-done.5.other_ref = bf16[256,1024]{1,0:T(8,128)(2,1)S(1)} collective-permute-done((bf16[256,1024]{1,0:T(8,128)(2,1)S(1)}, bf16[256,1024]{1,0:T(8,128)(2,1)S(1)}, u32[]{:S(2)}, u32[]{:S(2)}) %collective-permute-start.5) | collective-permute-done | bytes 524320 | tf_op jit(solution)/shard_map/ppermute | solution.py:203
  60.5 6.3 %shard_map.107 = bf16[32,8,1792]{2,1,0:T(8,128)(2,1)} custom-call(s32[1]{0:T(128)} %bitcast.2.core_ref, bf16[256,1024]{1,0:T(8,128)(2,1)S(1)} %pad_maximum_fusion.own_ref, bf16[256,1024]{1,0:T(8,128)(2,1)S(1)} %collective-permute-done.5.other_ref, bf16[1792,2,2048]{2,1,0:T(2,128)(2,1)S(1)} %bitcast.11, bf16[128,1792]{1,0:T(8,128)(2,1)S(1)} %shard_map.106.eo_ref), custom_call_target="tpu_custom_call" | custom-call | flops 3758096384 | bytes 14680064 | tf_op jit(solution)/shard_map/pallas_call | solution.py:307
  66.8 6.0 %all-to-all-start.2 = ((bf16[32,8,1792]{2,1,0:T(8,128)(2,1)}), bf16[32,8,1792]{2,1,0:T(8,128)(2,1)}, u32[]{:S(2)}, u32[]{:S(2)}) async-start(bf16[32,8,1792]{2,1,0:T(8,128)(2,1)} %shard_map.107), calls=%async_computation.2 | async-start | bytes 1835008 | tf_op jit(solution)/shard_map/all_to_all | solution.py:99
  72.8 0.9 copy-done.1
  73.8 0.9 copy-done.4
  74.7 4.6 %shard_map.110 = bf16[2048,1792]{1,0:T(8,128)(2,1)} custom-call(s32[1]{0:T(128)} %bitcast.2.core_ref, bf16[128,1024]{1,0:T(8,128)(2,1)S(1)} %copy-done.1, bf16[128,1024]{1,0:T(8,128)(2,1)S(1)} %copy-done.4, bf16[32,4,1792]{2,1,0:T(4,128)(2,1)S(1)} %all-to-all-done.1.sc_ref), custom_call_target="tpu_custom_call" | custom-call | flops 939524096 | bytes 7340032 | tf_op jit(solution)/shard_map/pallas_call | solution.py:392
  79.4 7.9 %shard_map.109 = bf16[1792,2,2048]{2,1,0:T(2,128)(2,1)} custom-call(s32[1]{0:T(128)} %bitcast.2.core_ref, bf16[256,1024]{1,0:T(8,128)(2,1)S(1)} %pad_maximum_fusion.own_ref, bf16[256,1024]{1,0:T(8,128)(2,1)S(1)} %collective-permute-done.5.other_ref, bf16[256,3584]{1,0:T(8,128)(2,1)S(1)} %get-tuple-element.32.spread_ref), custom_call_target="tpu_custom_call" | custom-call | flops 3758096384 | bytes 14680064 | tf_op jit(solution)/shard_map/pallas_call | solution.py:357
  87.3 10.3 %all-to-all-done.2.rows_hbm = bf16[32,8,1792]{2,1,0:T(8,128)(2,1)} async-done(((bf16[32,8,1792]{2,1,0:T(8,128)(2,1)}), bf16[32,8,1792]{2,1,0:T(8,128)(2,1)}, u32[]{:S(2)}, u32[]{:S(2)}) %all-to-all-start.2) | async-done | bytes 917536 | tf_op jit(solution)/shard_map/all_to_all | solution.py:99
  97.6 2.6 %shard_map.108 = (bf16[8,7168]{1,0:T(8,128)(2,1)}, bf16[8,7168]{1,0:T(8,128)(2,1)}, f32[4,8]{1,0:T(4,128)}) custom-call(s32[4,8]{1,0:T(4,128)S(1)} %bitcast.14, bf16[4,8]{1,0:T(4,128)(2,1)S(1)} %bitcast.17, bf16[8,7168]{1,0:T(8,128)(2,1)S(1)} %copy-done.2, bf16[32,8,1792]{2,1,0:T(8,128)(2,1)} %all-to-all-done.2.rows_hbm), custom_call_target="tpu_custom_call" | custom-call | flops 22020096 | bytes 917504 | tf_op jit(solution)/shard_map/pallas_call | solution.py:438
  (24 shorter events, 0.1 us)
Async XLA Ops:
  2.6 22.3 %all-to-all-start = ((bf16[32,4,1792]{2,1,0:T(4,128)(2,1)}), bf16[32,4,1792]{2,1,0:T(4,128)(2,1)S(1)}, u32[]{:S(2)}, u32[]{:S(2)}) async-start(bf16[32,4,1792]{2,1,0:T(4,128)(2,1)} %shard_map.101), calls=%async_computation | async-start | bytes 917504 | tf_op jit(solution)/shard_map/all_to_all | solution.py:99
  24.9 17.6 %all-to-all-start.1 = ((bf16[32,4,1792]{2,1,0:T(4,128)(2,1)}), bf16[32,4,1792]{2,1,0:T(4,128)(2,1)S(1)}, u32[]{:S(2)}, u32[]{:S(2)}) async-start(bf16[32,4,1792]{2,1,0:T(4,128)(2,1)} %shard_map.102), calls=%async_computation.1 | async-start | bytes 917504 | tf_op jit(solution)/shard_map/all_to_all | solution.py:99
  34.5 2.0 %collective-permute-start = (bf16[256,1024]{1,0:T(8,128)(2,1)S(1)}, bf16[256,1024]{1,0:T(8,128)(2,1)S(1)}, u32[]{:S(2)}, u32[]{:S(2)}) collective-permute-start(bf16[256,1024]{1,0:T(8,128)(2,1)S(1)} %get-tuple-element.21), channel_id=1, source_target_pairs={{0,8},{8,0},{16,24},{24,16},{1,9},{9,1},{17,25},{25,17},{2,10},{10... | collective-permute-start | bytes 1572872 | tf_op jit(solution)/shard_map/ppermute | solution.py:203
  36.6 14.8 %collective-permute-start.1 = (bf16[256,1024]{1,0:T(8,128)(2,1)S(1)}, bf16[256,1024]{1,0:T(8,128)(2,1)S(1)}, u32[]{:S(2)}, u32[]{:S(2)}) collective-permute-start(bf16[256,1024]{1,0:T(8,128)(2,1)S(1)} %add_convert_fusion.refs_0_), channel_id=1, source_target_pairs={{0,16},{8,24},{16,0},{24,8},{1,17},{9,25},{17,1},{25,9},{2,18},{10... | collective-permute-start | bytes 1572872 | tf_op jit(solution)/shard_map/ppermute | solution.py:213
  42.4 18.0 %slice-start = ((s8[14680064]{0:T(1024)(128)(4,1)}), s8[4194304]{0:T(1024)(128)(4,1)S(1)}, s32[]{:S(2)}) async-start(s8[14680064]{0:T(1024)(128)(4,1)} %bitcast.9), calls=%async_computation.3 | async-start | bytes 8388608
  47.3 1.6 %collective-permute-start.2 = (bf16[128,1024]{1,0:T(8,128)(2,1)S(1)}, bf16[128,1024]{1,0:T(8,128)(2,1)S(1)}, u32[]{:S(2)}, u32[]{:S(2)}) collective-permute-start(bf16[128,1024]{1,0:T(8,128)(2,1)S(1)} %get-tuple-element.24), channel_id=1, source_target_pairs={{0,8},{8,0},{16,24},{24,16},{1,9},{9,1},{17,25},{25,17},{2,10},{10... | collective-permute-start | bytes 786440 | tf_op jit(solution)/shard_map/ppermute | solution.py:203
  48.9 11.6 %slice-start.1 = ((s8[14680064]{0:T(1024)(128)(4,1)}), s8[4194304]{0:T(1024)(128)(4,1)S(1)}, s32[]{:S(2)}) async-start(s8[14680064]{0:T(1024)(128)(4,1)} %bitcast.9), calls=%async_computation.4 | async-start | bytes 8388608
  48.9 9.2 %collective-permute-start.3 = (bf16[128,1024]{1,0:T(8,128)(2,1)S(1)}, bf16[128,1024]{1,0:T(8,128)(2,1)S(1)}, u32[]{:S(2)}, u32[]{:S(2)}) collective-permute-start(bf16[128,1024]{1,0:T(8,128)(2,1)S(1)} %add_convert_fusion.1), channel_id=1, source_target_pairs={{0,16},{8,24},{16,0},{24,8},{1,17},{9,25},{17,1},{25,9},{2,18},{10... | collective-permute-start | bytes 786440 | tf_op jit(solution)/shard_map/ppermute | solution.py:213
  51.6 6.5 %copy-start = (bf16[128,1024]{1,0:T(8,128)(2,1)}, bf16[128,1024]{1,0:T(8,128)(2,1)S(1)}, u32[]{:S(2)}) copy-start(bf16[128,1024]{1,0:T(8,128)(2,1)S(1)} %shard_map.105.own_ref) | copy-start | bytes 786436
  51.6 1.6 %collective-permute-start.4 = (bf16[128,1024]{1,0:T(8,128)(2,1)S(1)}, bf16[128,1024]{1,0:T(8,128)(2,1)S(1)}, u32[]{:S(2)}, u32[]{:S(2)}) collective-permute-start(bf16[128,1024]{1,0:T(8,128)(2,1)S(1)} %shard_map.105.own_ref), channel_id=1, source_target_pairs={{0,8},{8,0},{16,24},{24,16},{1,9},{9,1},{17,25},{25,17},{2,10},{10... | collective-permute-start | bytes 786440 | tf_op jit(solution)/shard_map/ppermute | solution.py:203
  51.9 8.6 %slice-start.2 = ((s8[14680064]{0:T(1024)(128)(4,1)}), s8[4194304]{0:T(1024)(128)(4,1)S(1)}, s32[]{:S(2)}) async-start(s8[14680064]{0:T(1024)(128)(4,1)} %bitcast.9), calls=%async_computation.5 | async-start | bytes 8388608
  51.9 8.6 %slice-start.3 = ((s8[14680064]{0:T(1024)(128)(4,1)}), s8[2097152]{0:T(1024)(128)(4,1)S(1)}, s32[]{:S(2)}) async-start(s8[14680064]{0:T(1024)(128)(4,1)} %bitcast.9), calls=%async_computation.6 | async-start | bytes 4194304
  53.2 4.9 %copy-start.3 = (bf16[128,1024]{1,0:T(8,128)(2,1)}, bf16[128,1024]{1,0:T(8,128)(2,1)S(1)}, u32[]{:S(2)}) copy-start(bf16[128,1024]{1,0:T(8,128)(2,1)S(1)} %collective-permute-done.4.other_ref) | copy-start | bytes 786436
  58.5 2.0 %collective-permute-start.5 = (bf16[256,1024]{1,0:T(8,128)(2,1)S(1)}, bf16[256,1024]{1,0:T(8,128)(2,1)S(1)}, u32[]{:S(2)}, u32[]{:S(2)}) collective-permute-start(bf16[256,1024]{1,0:T(8,128)(2,1)S(1)} %pad_maximum_fusion.own_ref), channel_id=1, source_target_pairs={{0,8},{8,0},{16,24},{24,16},{1,9},{9,1},{17,25},{25,17},{2,10},{10... | collective-permute-start | bytes 1572872 | tf_op jit(solution)/shard_map/ppermute | solution.py:203
  66.8 30.8 %all-to-all-start.2 = ((bf16[32,8,1792]{2,1,0:T(8,128)(2,1)}), bf16[32,8,1792]{2,1,0:T(8,128)(2,1)}, u32[]{:S(2)}, u32[]{:S(2)}) async-start(bf16[32,8,1792]{2,1,0:T(8,128)(2,1)} %shard_map.107), calls=%async_computation.2 | async-start | bytes 1835008 | tf_op jit(solution)/shard_map/all_to_all | solution.py:99
  72.8 1.0 copy-start.1
  73.8 0.9 copy-start.4
  79.3 18.3 %copy-start.2 = (bf16[8,7168]{1,0:T(8,128)(2,1)S(1)}, bf16[8,7168]{1,0:T(8,128)(2,1)}, u32[]{:S(2)}) copy-start(bf16[8,7168]{1,0:T(8,128)(2,1)} %cot_ref.1) | copy-start | bytes 344068
  79.4 18.2 %copy-start.5 = (s32[8,4]{0,1:T(4,128)S(1)}, s32[8,4]{0,1:T(4,128)}, u32[]{:S(2)}) copy-start(s32[8,4]{0,1:T(4,128)} %param.7) | copy-start | bytes 388
  79.4 18.2 %copy-start.6 = (bf16[8,4]{0,1:T(4,128)(2,1)S(1)}, bf16[8,4]{0,1:T(4,128)(2,1)}, u32[]{:S(2)}) copy-start(bf16[8,4]{0,1:T(4,128)(2,1)} %param.8) | copy-start | bytes 196

commit v4 on v3

--- a/solution.py
+++ b/solution.py
@@ -99,7 +99,7 @@
     return lax.all_to_all(rows, BOTH, split_axis=0, concat_axis=0, tiled=True)
 
 
-def stream(copies, ahead=2):
+def stream(copies, ahead=4):
     for copy in copies[:ahead]:
         copy.start()
 

time: 101 us -> 99.8 us (0.988)
  Pallas kernels: 42.3 us -> 41.1 us
  transfers between devices with their start and end apart: 9 -> 9, of which waited for: 8 -> 8; matrix products, arithmetic and copies ran while one was open for 0% -> 0% of each run, Pallas kernels for 31% -> 30%
where the time goes in v4:
time: 99.8 us; the launch traced here: 99.3 us
  Pallas kernels  41.1 us (41%)
  waiting for transfers between devices  36.1 us (36%)
  starting transfers between devices  18.5 us (19%)
  local copies, waits for them, and re-layouts  1.94 us (2%)
    all_to_all x3, waiting for transfers between devices, exchange(): return lax.all_to_all(rows, BOTH, split_axis=0, concat_axis=0, tiled=True)  27.7 us
    all_to_all x3, starting transfers between devices, exchange(): return lax.all_to_all(rows, BOTH, split_axis=0, concat_axis=0, tiled=True)  15.8 us
    pallas_call x1, Pallas kernels, grad_in(): pl.pallas_call(grad_in_kernel, in_specs=[SMEM, VMEM, VMEM, VMEM], out_spe...  7.9 us
    pallas_call x1, Pallas kernels, pre_halves(): pl.pallas_call(pre_kernel, in_specs=[SMEM, VMEM, HBM], out_specs=[VMEM, V...  6.65 us
    ppermute x4, waiting for transfers between devices, swap_cores(): return lax.ppermute(value, 'erow', [(i, i ^ 1) for i in range(n_row)])  6.47 us
    pallas_call x1, Pallas kernels, grad_rows(): pl.pallas_call(functools.partial(grad_rows_kernel, steps), in_specs=[SMEM...  6.3 us
    pallas_call x1, Pallas kernels, grad_out(): pl.pallas_call(grad_out_kernel, in_specs=[SMEM, VMEM, VMEM, VMEM], out_sp...  4.61 us
    pallas_call x1, Pallas kernels, down_t_halves(): pl.pallas_call(down_t_kernel, in_specs=[SMEM, VMEM, HBM], out_specs=[VMEM...  4.58 us
  transfers between devices with their start and end apart: 9, of which 8 were waited for; matrix products, arithmetic and copies ran while one was open for 0% of the time, Pallas kernels for 30%

profile of v4, /device:TPU:0, one launch (start us, length us, event | category | flops | bytes accessed | tf_op | source)
XLA Modules:
  0.0 99.3 jit_solution(6260771957917022604)
XLA Ops:
  0.6 2.0 %shard_map.101 = bf16[32,4,1792]{2,1,0:T(4,128)(2,1)} custom-call(s32[4,8]{1,0:T(4,128)} %bitcast.12, bf16[4,8]{1,0:T(4,128)(2,1)} %bitcast.15, bf16[8,7168]{1,0:T(8,128)(2,1)} %rows_hbm.2), custom_call_target="tpu_custom_call" | custom-call | flops 3670016 | bytes 114688 | tf_op jit(solution)/shard_map/pallas_call | solution.py:83
  2.6 7.3 %all-to-all-start = ((bf16[32,4,1792]{2,1,0:T(4,128)(2,1)}), bf16[32,4,1792]{2,1,0:T(4,128)(2,1)S(1)}, u32[]{:S(2)}, u32[]{:S(2)}) async-start(bf16[32,4,1792]{2,1,0:T(4,128)(2,1)} %shard_map.101), calls=%async_computation | async-start | bytes 917504 | tf_op jit(solution)/shard_map/all_to_all | solution.py:99
  9.9 2.0 %shard_map.102 = bf16[32,4,1792]{2,1,0:T(4,128)(2,1)} custom-call(s32[4,8]{1,0:T(4,128)} %bitcast.13, bf16[4,8]{1,0:T(4,128)(2,1)} %bitcast.16, bf16[8,7168]{1,0:T(8,128)(2,1)} %cot_ref.1), custom_call_target="tpu_custom_call" | custom-call | flops 3670016 | bytes 114688 | tf_op jit(solution)/shard_map/pallas_call | solution.py:83
  11.9 13.0 %all-to-all-done.x_ref = bf16[32,4,1792]{2,1,0:T(4,128)(2,1)S(1)} async-done(((bf16[32,4,1792]{2,1,0:T(4,128)(2,1)}), bf16[32,4,1792]{2,1,0:T(4,128)(2,1)S(1)}, u32[]{:S(2)}, u32[]{:S(2)}) %all-to-all-start) | async-done | bytes 458784 | tf_op jit(solution)/shard_map/all_to_all | solution.py:99
  24.9 2.6 %all-to-all-start.1 = ((bf16[32,4,1792]{2,1,0:T(4,128)(2,1)}), bf16[32,4,1792]{2,1,0:T(4,128)(2,1)S(1)}, u32[]{:S(2)}, u32[]{:S(2)}) async-start(bf16[32,4,1792]{2,1,0:T(4,128)(2,1)} %shard_map.102), calls=%async_computation.1 | async-start | bytes 917504 | tf_op jit(solution)/shard_map/all_to_all | solution.py:99
  27.5 6.7 %shard_map.103 = (bf16[256,1024]{1,0:T(8,128)(2,1)S(1)}, f32[256,1024]{1,0:T(8,128)S(1)}, bf16[256,3584]{1,0:T(8,128)(2,1)S(1)}) custom-call(s32[1]{0:T(128)} %bitcast.2.core_ref, bf16[32,4,1792]{2,1,0:T(4,128)(2,1)S(1)} %all-to-all-done.x_ref, bf16[1792,2,2048]{2,1,0:T(2,128)(2,1)} %bitcast.8), custom_call_target="tpu_custom_call" | custom-call | flops 10000000000 | bytes 14680064 | tf_op jit(solution)/shard_map/pallas_call | solution.py:147
  34.1 0.2 collective-permute-start
  34.3 1.8 %collective-permute-done = bf16[256,1024]{1,0:T(8,128)(2,1)S(1)} collective-permute-done((bf16[256,1024]{1,0:T(8,128)(2,1)S(1)}, bf16[256,1024]{1,0:T(8,128)(2,1)S(1)}, u32[]{:S(2)}, u32[]{:S(2)}) %collective-permute-start) | collective-permute-done | bytes 524320 | tf_op jit(solution)/shard_map/ppermute | solution.py:203
  36.1 0.2 add_convert_fusion.refs_0_
  36.3 1.7 %collective-permute-start.1 = (bf16[256,1024]{1,0:T(8,128)(2,1)S(1)}, bf16[256,1024]{1,0:T(8,128)(2,1)S(1)}, u32[]{:S(2)}, u32[]{:S(2)}) collective-permute-start(bf16[256,1024]{1,0:T(8,128)(2,1)S(1)} %add_convert_fusion.refs_0_), channel_id=1, source_target_pairs={{0,16},{8,24},{16,0},{24,8},{1,17},{9,25},{17,1},{25,9},{2,18},{10... | collective-permute-start | bytes 1572872 | tf_op jit(solution)/shard_map/ppermute | solution.py:213
  38.0 4.5 %all-to-all-done.1.sc_ref = bf16[32,4,1792]{2,1,0:T(4,128)(2,1)S(1)} async-done(((bf16[32,4,1792]{2,1,0:T(4,128)(2,1)}), bf16[32,4,1792]{2,1,0:T(4,128)(2,1)S(1)}, u32[]{:S(2)}, u32[]{:S(2)}) %all-to-all-start.1) | async-done | bytes 458784 | tf_op jit(solution)/shard_map/all_to_all | solution.py:99
  42.4 4.6 %shard_map.104 = (bf16[128,1024]{1,0:T(8,128)(2,1)S(1)}, f32[128,1024]{1,0:T(8,128)S(1)}) custom-call(s32[1]{0:T(128)} %bitcast.2.core_ref, bf16[32,4,1792]{2,1,0:T(4,128)(2,1)S(1)} %all-to-all-done.1.sc_ref, bf16[2048,1792]{1,0:T(8,128)(2,1)} %bitcast.19), custom_call_target="tpu_custom_call" | custom-call | flops 939524096 | bytes 7340032 | tf_op jit(solution)/shard_map/pallas_call | solution.py:187
  47.0 0.1 collective-permute-start.2
  47.1 1.5 %collective-permute-done.2 = bf16[128,1024]{1,0:T(8,128)(2,1)S(1)} collective-permute-done((bf16[128,1024]{1,0:T(8,128)(2,1)S(1)}, bf16[128,1024]{1,0:T(8,128)(2,1)S(1)}, u32[]{:S(2)}, u32[]{:S(2)}) %collective-permute-start.2) | collective-permute-done | bytes 262176 | tf_op jit(solution)/shard_map/ppermute | solution.py:203
  48.7 0.6 collective-permute-start.3
  49.3 1.9 %collective-permute-done.1.refs_1_ = bf16[256,1024]{1,0:T(8,128)(2,1)S(1)} collective-permute-done((bf16[256,1024]{1,0:T(8,128)(2,1)S(1)}, bf16[256,1024]{1,0:T(8,128)(2,1)S(1)}, u32[]{:S(2)}, u32[]{:S(2)}) %collective-permute-start.1) | collective-permute-done | bytes 524320 | tf_op jit(solution)/shard_map/ppermute | solution.py:213
  51.2 0.2 shard_map.105.own_ref
  51.4 0.1 collective-permute-start.4
  51.5 0.2 convert_add_fusion
  51.7 1.3 %collective-permute-done.4.other_ref = bf16[128,1024]{1,0:T(8,128)(2,1)S(1)} collective-permute-done((bf16[128,1024]{1,0:T(8,128)(2,1)S(1)}, bf16[128,1024]{1,0:T(8,128)(2,1)S(1)}, u32[]{:S(2)}, u32[]{:S(2)}) %collective-permute-start.4) | collective-permute-done | bytes 262176 | tf_op jit(solution)/shard_map/ppermute | solution.py:203
  53.0 4.3 %shard_map.106.eo_ref = bf16[128,1792]{1,0:T(8,128)(2,1)S(1)} custom-call(s32[1]{0:T(128)} %bitcast.2.core_ref, bf16[128,1024]{1,0:T(8,128)(2,1)S(1)} %shard_map.105.own_ref, bf16[128,1024]{1,0:T(8,128)(2,1)S(1)} %collective-permute-done.4.other_ref, bf16[2048,1792]{1,0:T(8,128)(2,1)} %bitcast.20), custom_call_target="tpu_custom_call" | custom-call | flops 5000000000 | bytes 7340032 | tf_op jit(solution)/shard_map/pallas_call | solution.py:260
  57.4 0.3 fusion.2
  57.7 0.2 collective-permute-start.5
  57.9 1.8 %collective-permute-done.5.other_ref = bf16[256,1024]{1,0:T(8,128)(2,1)S(1)} collective-permute-done((bf16[256,1024]{1,0:T(8,128)(2,1)S(1)}, bf16[256,1024]{1,0:T(8,128)(2,1)S(1)}, u32[]{:S(2)}, u32[]{:S(2)}) %collective-permute-start.5) | collective-permute-done | bytes 524320 | tf_op jit(solution)/shard_map/ppermute | solution.py:203
  59.7 6.3 %shard_map.107 = bf16[32,8,1792]{2,1,0:T(8,128)(2,1)} custom-call(s32[1]{0:T(128)} %bitcast.2.core_ref, bf16[256,1024]{1,0:T(8,128)(2,1)S(1)} %pad_maximum_fusion.own_ref, bf16[256,1024]{1,0:T(8,128)(2,1)S(1)} %collective-permute-done.5.other_ref, bf16[1792,2,2048]{2,1,0:T(2,128)(2,1)S(1)} %bitcast.11, bf16[128,1792]{1,0:T(8,128)(2,1)S(1)} %shard_map.106.eo_ref), custom_call_target="tpu_custom_call" | custom-call | flops 3758096384 | bytes 14680064 | tf_op jit(solution)/shard_map/pallas_call | solution.py:307
  66.0 5.9 %all-to-all-start.2 = ((bf16[32,8,1792]{2,1,0:T(8,128)(2,1)}), bf16[32,8,1792]{2,1,0:T(8,128)(2,1)}, u32[]{:S(2)}, u32[]{:S(2)}) async-start(bf16[32,8,1792]{2,1,0:T(8,128)(2,1)} %shard_map.107), calls=%async_computation.2 | async-start | bytes 1835008 | tf_op jit(solution)/shard_map/all_to_all | solution.py:99
  71.9 0.9 copy-done.1
  72.9 0.9 copy-done.4
  73.8 4.6 %shard_map.110 = bf16[2048,1792]{1,0:T(8,128)(2,1)} custom-call(s32[1]{0:T(128)} %bitcast.2.core_ref, bf16[128,1024]{1,0:T(8,128)(2,1)S(1)} %copy-done.1, bf16[128,1024]{1,0:T(8,128)(2,1)S(1)} %copy-done.4, bf16[32,4,1792]{2,1,0:T(4,128)(2,1)S(1)} %all-to-all-done.1.sc_ref), custom_call_target="tpu_custom_call" | custom-call | flops 939524096 | bytes 7340032 | tf_op jit(solution)/shard_map/pallas_call | solution.py:392
  78.5 7.9 %shard_map.109 = bf16[1792,2,2048]{2,1,0:T(2,128)(2,1)} custom-call(s32[1]{0:T(128)} %bitcast.2.core_ref, bf16[256,1024]{1,0:T(8,128)(2,1)S(1)} %pad_maximum_fusion.own_ref, bf16[256,1024]{1,0:T(8,128)(2,1)S(1)} %collective-permute-done.5.other_ref, bf16[256,3584]{1,0:T(8,128)(2,1)S(1)} %get-tuple-element.32.spread_ref), custom_call_target="tpu_custom_call" | custom-call | flops 3758096384 | bytes 14680064 | tf_op jit(solution)/shard_map/pallas_call | solution.py:357
  86.4 10.3 %all-to-all-done.2.rows_hbm = bf16[32,8,1792]{2,1,0:T(8,128)(2,1)} async-done(((bf16[32,8,1792]{2,1,0:T(8,128)(2,1)}), bf16[32,8,1792]{2,1,0:T(8,128)(2,1)}, u32[]{:S(2)}, u32[]{:S(2)}) %all-to-all-start.2) | async-done | bytes 917536 | tf_op jit(solution)/shard_map/all_to_all | solution.py:99
  96.7 2.6 %shard_map.108 = (bf16[8,7168]{1,0:T(8,128)(2,1)}, bf16[8,7168]{1,0:T(8,128)(2,1)}, f32[4,8]{1,0:T(4,128)}) custom-call(s32[4,8]{1,0:T(4,128)S(1)} %bitcast.14, bf16[4,8]{1,0:T(4,128)(2,1)S(1)} %bitcast.17, bf16[8,7168]{1,0:T(8,128)(2,1)S(1)} %copy-done.2, bf16[32,8,1792]{2,1,0:T(8,128)(2,1)} %all-to-all-done.2.rows_hbm), custom_call_target="tpu_custom_call" | custom-call | flops 22020096 | bytes 917504 | tf_op jit(solution)/shard_map/pallas_call | solution.py:438
  (24 shorter events, 0.1 us)
Async XLA Ops:
  2.6 22.3 %all-to-all-start = ((bf16[32,4,1792]{2,1,0:T(4,128)(2,1)}), bf16[32,4,1792]{2,1,0:T(4,128)(2,1)S(1)}, u32[]{:S(2)}, u32[]{:S(2)}) async-start(bf16[32,4,1792]{2,1,0:T(4,128)(2,1)} %shard_map.101), calls=%async_computation | async-start | bytes 917504 | tf_op jit(solution)/shard_map/all_to_all | solution.py:99
  24.9 17.6 %all-to-all-start.1 = ((bf16[32,4,1792]{2,1,0:T(4,128)(2,1)}), bf16[32,4,1792]{2,1,0:T(4,128)(2,1)S(1)}, u32[]{:S(2)}, u32[]{:S(2)}) async-start(bf16[32,4,1792]{2,1,0:T(4,128)(2,1)} %shard_map.102), calls=%async_computation.1 | async-start | bytes 917504 | tf_op jit(solution)/shard_map/all_to_all | solution.py:99
  34.1 2.0 %collective-permute-start = (bf16[256,1024]{1,0:T(8,128)(2,1)S(1)}, bf16[256,1024]{1,0:T(8,128)(2,1)S(1)}, u32[]{:S(2)}, u32[]{:S(2)}) collective-permute-start(bf16[256,1024]{1,0:T(8,128)(2,1)S(1)} %get-tuple-element.21), channel_id=1, source_target_pairs={{0,8},{8,0},{16,24},{24,16},{1,9},{9,1},{17,25},{25,17},{2,10},{10... | collective-permute-start | bytes 1572872 | tf_op jit(solution)/shard_map/ppermute | solution.py:203
  36.3 14.9 %collective-permute-start.1 = (bf16[256,1024]{1,0:T(8,128)(2,1)S(1)}, bf16[256,1024]{1,0:T(8,128)(2,1)S(1)}, u32[]{:S(2)}, u32[]{:S(2)}) collective-permute-start(bf16[256,1024]{1,0:T(8,128)(2,1)S(1)} %add_convert_fusion.refs_0_), channel_id=1, source_target_pairs={{0,16},{8,24},{16,0},{24,8},{1,17},{9,25},{17,1},{25,9},{2,18},{10... | collective-permute-start | bytes 1572872 | tf_op jit(solution)/shard_map/ppermute | solution.py:213
  42.4 17.3 %slice-start = ((s8[14680064]{0:T(1024)(128)(4,1)}), s8[4194304]{0:T(1024)(128)(4,1)S(1)}, s32[]{:S(2)}) async-start(s8[14680064]{0:T(1024)(128)(4,1)} %bitcast.9), calls=%async_computation.3 | async-start | bytes 8388608
  47.0 1.6 %collective-permute-start.2 = (bf16[128,1024]{1,0:T(8,128)(2,1)S(1)}, bf16[128,1024]{1,0:T(8,128)(2,1)S(1)}, u32[]{:S(2)}, u32[]{:S(2)}) collective-permute-start(bf16[128,1024]{1,0:T(8,128)(2,1)S(1)} %get-tuple-element.24), channel_id=1, source_target_pairs={{0,8},{8,0},{16,24},{24,16},{1,9},{9,1},{17,25},{25,17},{2,10},{10... | collective-permute-start | bytes 786440 | tf_op jit(solution)/shard_map/ppermute | solution.py:203
  48.6 11.1 %slice-start.1 = ((s8[14680064]{0:T(1024)(128)(4,1)}), s8[4194304]{0:T(1024)(128)(4,1)S(1)}, s32[]{:S(2)}) async-start(s8[14680064]{0:T(1024)(128)(4,1)} %bitcast.9), calls=%async_computation.4 | async-start | bytes 8388608
  48.7 8.7 %collective-permute-start.3 = (bf16[128,1024]{1,0:T(8,128)(2,1)S(1)}, bf16[128,1024]{1,0:T(8,128)(2,1)S(1)}, u32[]{:S(2)}, u32[]{:S(2)}) collective-permute-start(bf16[128,1024]{1,0:T(8,128)(2,1)S(1)} %add_convert_fusion.1), channel_id=1, source_target_pairs={{0,16},{8,24},{16,0},{24,8},{1,17},{9,25},{17,1},{25,9},{2,18},{10... | collective-permute-start | bytes 786440 | tf_op jit(solution)/shard_map/ppermute | solution.py:213
  51.4 5.9 %copy-start = (bf16[128,1024]{1,0:T(8,128)(2,1)}, bf16[128,1024]{1,0:T(8,128)(2,1)S(1)}, u32[]{:S(2)}) copy-start(bf16[128,1024]{1,0:T(8,128)(2,1)S(1)} %shard_map.105.own_ref) | copy-start | bytes 786436
  51.4 1.6 %collective-permute-start.4 = (bf16[128,1024]{1,0:T(8,128)(2,1)S(1)}, bf16[128,1024]{1,0:T(8,128)(2,1)S(1)}, u32[]{:S(2)}, u32[]{:S(2)}) collective-permute-start(bf16[128,1024]{1,0:T(8,128)(2,1)S(1)} %shard_map.105.own_ref), channel_id=1, source_target_pairs={{0,8},{8,0},{16,24},{24,16},{1,9},{9,1},{17,25},{25,17},{2,10},{10... | collective-permute-start | bytes 786440 | tf_op jit(solution)/shard_map/ppermute | solution.py:203
  51.7 8.0 %slice-start.2 = ((s8[14680064]{0:T(1024)(128)(4,1)}), s8[4194304]{0:T(1024)(128)(4,1)S(1)}, s32[]{:S(2)}) async-start(s8[14680064]{0:T(1024)(128)(4,1)} %bitcast.9), calls=%async_computation.5 | async-start | bytes 8388608
  51.7 8.0 %slice-start.3 = ((s8[14680064]{0:T(1024)(128)(4,1)}), s8[2097152]{0:T(1024)(128)(4,1)S(1)}, s32[]{:S(2)}) async-start(s8[14680064]{0:T(1024)(128)(4,1)} %bitcast.9), calls=%async_computation.6 | async-start | bytes 4194304
  53.0 4.3 %copy-start.3 = (bf16[128,1024]{1,0:T(8,128)(2,1)}, bf16[128,1024]{1,0:T(8,128)(2,1)S(1)}, u32[]{:S(2)}) copy-start(bf16[128,1024]{1,0:T(8,128)(2,1)S(1)} %collective-permute-done.4.other_ref) | copy-start | bytes 786436
  57.7 2.0 %collective-permute-start.5 = (bf16[256,1024]{1,0:T(8,128)(2,1)S(1)}, bf16[256,1024]{1,0:T(8,128)(2,1)S(1)}, u32[]{:S(2)}, u32[]{:S(2)}) collective-permute-start(bf16[256,1024]{1,0:T(8,128)(2,1)S(1)} %pad_maximum_fusion.own_ref), channel_id=1, source_target_pairs={{0,8},{8,0},{16,24},{24,16},{1,9},{9,1},{17,25},{25,17},{2,10},{10... | collective-permute-start | bytes 1572872 | tf_op jit(solution)/shard_map/ppermute | solution.py:203
  66.0 30.6 %all-to-all-start.2 = ((bf16[32,8,1792]{2,1,0:T(8,128)(2,1)}), bf16[32,8,1792]{2,1,0:T(8,128)(2,1)}, u32[]{:S(2)}, u32[]{:S(2)}) async-start(bf16[32,8,1792]{2,1,0:T(8,128)(2,1)} %shard_map.107), calls=%async_computation.2 | async-start | bytes 1835008 | tf_op jit(solution)/shard_map/all_to_all | solution.py:99
  71.9 1.0 copy-start.1
  72.9 0.9 copy-start.4
  78.4 18.3 %copy-start.2 = (bf16[8,7168]{1,0:T(8,128)(2,1)S(1)}, bf16[8,7168]{1,0:T(8,128)(2,1)}, u32[]{:S(2)}) copy-start(bf16[8,7168]{1,0:T(8,128)(2,1)} %cot_ref.1) | copy-start | bytes 344068
  78.4 18.2 %copy-start.5 = (s32[8,4]{0,1:T(4,128)S(1)}, s32[8,4]{0,1:T(4,128)}, u32[]{:S(2)}) copy-start(s32[8,4]{0,1:T(4,128)} %param.7) | copy-start | bytes 388
  78.4 18.2 %copy-start.6 = (bf16[8,4]{0,1:T(4,128)(2,1)S(1)}, bf16[8,4]{0,1:T(4,128)(2,1)}, u32[]{:S(2)}) copy-start(bf16[8,4]{0,1:T(4,128)(2,1)} %param.8) | copy-start | bytes 196
